TPU v7x, 32 devices: a whole 2x2x4 slice. The times are simulated.
32 devices in a mesh: dp: 8 (over z, y), mp: 4 (over x, core).
Axes of the slice: x: 2, y: 2, z: 4, core: 2. Of those that a mesh axis runs over, the one named last changes fastest.
Arguments:
- chars: int32 [4096, 50], P('dp'), may hold values from 0 to 261
- char_mask: int32 [4096, 50], P('dp'), may hold values from 0 to 1, as said below
- word_order: int32 [4096], replicated, may hold values from 0 to 4095, as said below
- segment_ids: int32 [8, 512], P('dp'), may hold values from 0 to 7, never falling along the last dimension, each value on 1 to 128 neighbouring positions
- char_table: float32 [262, 16], replicated, may hold values from -6 to 6
- conv_weight: bfloat16 [112, 2048], P(None, 'mp'), may hold values from -0.75 to 0.75
- conv_bias: float32 [2048], P('mp'), may hold values from -3 to 3
- highway_weight: bfloat16 [2, 2048, 2, 2048], P(None, None, None, 'mp'), may hold values from -0.125 to 0.125
- highway_bias: float32 [2, 2, 2048], P(None, None, 'mp'), may hold values from -3 to 3
- project_weight: bfloat16 [2048, 768], P('mp'), may hold values from -0.125 to 0.125
- project_bias: float32 [768], replicated, may hold values from -3 to 3
- position_table: float32 [512, 768], replicated, may hold values from -5 to 5
- norm_gain: float32 [3, 768], replicated, may hold values from 0.5 to 1.5
- norm_bias: float32 [3, 768], replicated, may hold values from -2 to 2
- qkv_weight: bfloat16 [768, 3, 768], P(None, None, 'mp'), may hold values from -0.21875 to 0.21875
- qv_bias: float32 [2, 768], P(None, 'mp'), may hold values from -2 to 2
- out_weight: bfloat16 [768, 768], P('mp'), may hold values from -0.875 to 0.875
- out_bias: float32 [768], replicated, may hold values from -2 to 2
- up_weight: bfloat16 [768, 3072], P(None, 'mp'), may hold values from -0.21875 to 0.21875
- up_bias: float32 [3072], P('mp'), may hold values from -2 to 2
- down_weight: bfloat16 [3072, 768], P('mp'), may hold values from -0.109375 to 0.109375
- down_bias: float32 [768], replicated, may hold values from -2 to 2
- out_grad: float32 [4096, 768], P('dp'), may hold values from -6 to 6
Outputs:
- encoded: float32 [4096, 768], P('dp')
- char_table_grad: float32 [262, 16], replicated
- conv_weight_grad: float32 [112, 2048], P(None, 'mp')
- conv_bias_grad: float32 [2048], P('mp')
- highway_weight_grad: float32 [2, 2048, 2, 2048], P(None, 'dp', None, 'mp')
- highway_bias_grad: float32 [2, 2, 2048], P(None, None, 'mp')
- project_weight_grad: float32 [2048, 768], P('mp', 'dp')
- project_bias_grad: float32 [768], replicated
- position_table_grad: float32 [512, 768], replicated
- norm_gain_grad: float32 [3, 768], replicated
- norm_bias_grad: float32 [3, 768], replicated
- qkv_weight_grad: float32 [768, 3, 768], P('dp', None, 'mp')
- qv_bias_grad: float32 [2, 768], P(None, 'mp')
- out_weight_grad: float32 [768, 768], P('mp', 'dp')
- out_bias_grad: float32 [768], replicated
- up_weight_grad: float32 [768, 3072], P('dp', 'mp')
- up_bias_grad: float32 [3072], P('mp')
- down_weight_grad: float32 [3072, 768], P('mp', 'dp')
- down_bias_grad: float32 [768], replicated
Inputs may be any that keep to these rules, and one draw needn't show every extreme that they name: `char_mask`: each slot's mask is 1 on its first l characters and 0 after, 1 <= l <= 50; some slot has l = 50. `word_order`: a permutation of the tokens; cut the slots that one index s of dp holds into 8 equal runs in order, numbered d from 0; run d holds exactly the tokens of a share of the rows that index d of dp holds, every token of those rows in some run d of some index s; over the runs d of all indices s, taken in the order of s, words have at least as many characters in later runs.
All inputs are finite; a program needn't handle non-finite values.
Results may differ from a plain program's by a relative error of at most 0.023.
Values may be sent and summed in bfloat16 or wider, within the bound.
No kernel may reach another device: no remote copies, remote signals or barrier semaphores. Data moves between devices by JAX's collectives and lax.ppermute only.
A program may use at most 192 MiB of HBM per device.

v0:
```python
import functools

import jax
import jax.numpy as jnp
from jax import lax
from jax.experimental import pallas as pl
from jax.experimental.pallas import tpu as pltpu
from jax.sharding import PartitionSpec as P

HEAD = 64
CHANNELS = 2048
CHAR_DIM = 16
CHARS = 50
TAPS = 7
LAYERS = 2
BLOCK = 128
TILES = 1

EPSILON = 1e-05
NEGATIVE = -1e30
F32 = jnp.float32
BF16 = jnp.bfloat16


def filter_mask(local_count, first):
    channel = first + jnp.arange(local_count, dtype=jnp.int32)
    tap_count = 1 + sum(
        ((channel >= CHANNELS // divisor).astype(jnp.int32) for divisor in (64, 32, 16, 8, 4, 2))
    )
    tap_index = jnp.arange(TAPS * CHAR_DIM, dtype=jnp.int32) // CHAR_DIM
    return tap_index[:, None] < tap_count[None, :]


STEPS = 8
ROWS = 7
SPAN = STEPS * CHAR_DIM
VMEM_LIMIT = 24 << 20
FREE = pl.CostEstimate(flops=1, bytes_accessed=1, transcendentals=0)

def spread_table(char_table):
    low = char_table.astype(BF16)
    eye = jnp.eye(STEPS, dtype=BF16)
    first = low[:256]
    rest = jnp.pad(low[256:], ((0, CHAR_DIM - (low.shape[0] - 256)), (0, 0)))
    parts = [(eye[:, None, :, None] * part[None, :, None, :]).reshape(-1, SPAN) for part in (first, rest)]
    return jnp.concatenate(parts, axis=0)

def place_filters(filters_ref, shifted):
    shifted[...] = jnp.zeros_like(shifted)
    taps = filters_ref.shape[0]
    width = filters_ref.shape[1]
    halved = (filters_ref[...].astype(F32) * 0.5).astype(BF16)
    for r in range(STEPS):
        shifted[CHAR_DIM * r : CHAR_DIM * r + taps, r * width : (r + 1) * width] = halved

def forward_kernel(block, counts, ids_ref, table_ref, filters_ref, bias_ref, pooled_ref, embed_ref, shifted, hot, total):
    words, width = pooled_ref.shape
    place_filters(filters_ref, shifted)
    lanes = lax.broadcasted_iota(jnp.int32, (words, 256), 1)
    lane = lax.broadcasted_iota(jnp.int32, (words, 128), 1)
    embed_ref[ROWS] = jnp.zeros_like(embed_ref[ROWS])
    total[...] = jnp.zeros_like(total)

    def embed(q, carry):
        left = jnp.zeros((words, 128), F32)
        for r in range(STEPS):
            ids = ids_ref[q, :, r : r + 1]
            hot[:, r * 256 : (r + 1) * 256] = jnp.where(ids == lanes, 1.0, 0.0).astype(BF16)
            mark = jnp.where(lane // CHAR_DIM == r, lane % CHAR_DIM + 256, -7)
            left = jnp.where(ids == mark, 1.0, left)
        hot[:, STEPS * 256 :] = left.astype(BF16)
        embed_ref[q] = jnp.dot(hot[...], table_ref[...], preferred_element_type=F32).astype(BF16)
        return carry

    lax.fori_loop(0, ROWS, embed, 0)
    half = bias_ref[...] * 0.5
    blocks = words // block

    def row(q, carry):
        def one(i, inner):
            rows = pl.ds(pl.multiple_of(i * block, block), block)
            x = jnp.concatenate([embed_ref[q, rows, :], embed_ref[q + 1, rows, :]], axis=1)
            for r in range(STEPS):
                u = jnp.dot(x, shifted[:, r * width : (r + 1) * width], preferred_element_type=F32) + half
                total[rows, :] += u + u * jnp.tanh(u)
            return inner

        lax.fori_loop(counts[blocks + q], blocks, one, 0)
        return carry

    lax.fori_loop(0, ROWS, row, 0)
    rest = half + half * jnp.tanh(half)
    for i in range(blocks):
        rows = slice(i * block, (i + 1) * block)
        seen = STEPS * counts[i]
        pooled_ref[rows, :] = (
            (total[rows, :] + (CHARS - seen).astype(F32) * rest) * (1.0 / CHARS)
        ).astype(BF16)


def block_counts(ids, block):
    most = jnp.max(jnp.sum((ids >= 0).astype(jnp.int32), axis=1).reshape(-1, block), axis=1)
    need = (most + STEPS - 1) // STEPS
    first = jnp.sum((need[None, :] <= jnp.arange(ROWS, dtype=jnp.int32)[:, None]).astype(jnp.int32), axis=1)
    return jnp.concatenate([need, first])

def cnn_forward(ids, counts, table, filters, bias, block):
    words = ids.shape[0]
    width = filters.shape[1]
    ids = jnp.pad(ids, ((0, 0), (0, ROWS * STEPS - CHARS)), constant_values=-1)
    ids = jnp.swapaxes(ids.reshape(words, ROWS, STEPS), 0, 1)
    vm = pl.BlockSpec(memory_space=pltpu.VMEM)
    return pl.pallas_call(
        functools.partial(forward_kernel, block),
        in_specs=[pl.BlockSpec(memory_space=pltpu.SMEM), vm, vm, vm, vm],
        out_specs=[vm, vm],
        out_shape=[jax.ShapeDtypeStruct((words, width), BF16), jax.ShapeDtypeStruct((ROWS + 1, words, SPAN), BF16)],
        scratch_shapes=[pltpu.VMEM((2 * SPAN, STEPS * width), BF16), pltpu.VMEM((words, STEPS * 256 + 128), BF16), pltpu.VMEM((words, width), F32)],
        compiler_params=pltpu.CompilerParams(vmem_limit_bytes=VMEM_LIMIT),
        cost_estimate=FREE,
    )(counts, ids, table, filters, bias.reshape(1, -1))


def backward_kernel(
    block,
    counts,
    embed_ref,
    filters_ref,
    bias_ref,
    grad_ref,
    embed_in,
    filter_out,
    bias_out,
    embed_grad,
    shifted,
    slopes,
    sums,
):
    words, width = grad_ref.shape
    blocks = words // block
    place_filters(filters_ref, shifted)
    half = bias_ref[...] * 0.5
    still = jnp.tanh(half)
    rest = (1.0 + still) + half * (1.0 - still * still)
    bias_out[...] = jnp.zeros_like(bias_out)
    sums[...] = jnp.zeros_like(sums)
    if embed_in is None:
        embed_grad[...] = jnp.zeros_like(embed_grad)
    else:
        embed_grad[...] = embed_in[...]
    scale = 0.5 / CHARS
    for i in range(blocks):
        grads = grad_ref[i * block : (i + 1) * block, :].astype(F32) * scale
        left = (CHARS - STEPS * counts[i]).astype(F32)
        bias_out[...] += jnp.sum(grads, axis=0, keepdims=True) * (rest * left)
    def row(q, outer):
        first = counts[blocks + q]

        def clear(i, carry):
            rows = pl.ds(pl.multiple_of(i * block, block), block)
            slopes[rows, :] = jnp.zeros((block, STEPS * width), BF16)
            return carry

        lax.fori_loop(counts[blocks + jnp.maximum(q - 1, 0)], first, clear, 0)

        def one(i, carry):
            rows = pl.ds(pl.multiple_of(i * block, block), block)
            x = jnp.concatenate([embed_ref[q, rows, :], embed_ref[q + 1, rows, :]], axis=1)
            grads = grad_ref[rows, :].astype(F32) * scale
            column = jnp.zeros((1, width), F32)
            for r in range(STEPS):
                cols = slice(r * width, (r + 1) * width)
                u = jnp.dot(x, shifted[:, cols], preferred_element_type=F32) + half
                t = jnp.tanh(u)
                slope = grads * ((1.0 + t) + u * (1.0 - t * t))
                column += jnp.sum(slope, axis=0, keepdims=True)
                slopes[rows, cols] = slope.astype(BF16)
            bias_out[...] += column
            return carry

        lax.fori_loop(first, blocks, one, 0)

        def spread(start):
            rows = slice(start, words)
            x = jnp.concatenate([embed_ref[q, rows, :], embed_ref[q + 1, rows, :]], axis=1)
            back = lax.dot_general(
                slopes[rows, :], shifted[...], (((1,), (1,)), ((), ())), preferred_element_type=F32
            )
            embed_grad[q, rows, :] += back[:, :SPAN]
            embed_grad[q + 1, rows, :] += back[:, SPAN:]
            for r in range(STEPS):
                cols = slice(r * width, (r + 1) * width)
                sums[:, cols] += lax.dot_general(
                    x, slopes[rows, cols], (((0,), (0,)), ((), ())), preferred_element_type=F32
                )

        middle = blocks // 2

        @pl.when(first < middle)
        def _():
            spread(0)

        @pl.when((first >= middle) & (first < blocks))
        def _():
            spread(middle * block)

        return outer

    lax.fori_loop(0, ROWS, row, 0)
    taps = filters_ref.shape[0]
    total = sums[:taps, :width]
    for r in range(1, STEPS):
        lower = CHAR_DIM * r
        total = total + sums[lower : lower + taps, r * width : (r + 1) * width]
    filter_out[...] = total


def cnn_backward(counts, embed, filters, bias, grad, embed_grad, block):
    words, width = grad.shape
    taps = filters.shape[0]
    vm = pl.BlockSpec(memory_space=pltpu.VMEM)
    operands = [counts, embed, filters, bias.reshape(1, -1), grad]
    kernel = functools.partial(backward_kernel, block)
    if embed_grad is None:
        inner = kernel

        def kernel(counts, embed, filters, bias, grad, *rest):
            inner(counts, embed, filters, bias, grad, None, *rest)
    else:
        operands.append(embed_grad)
    return pl.pallas_call(
        kernel,
        in_specs=[pl.BlockSpec(memory_space=pltpu.SMEM)] + [vm] * (len(operands) - 1),
        out_specs=[vm] * 3,
        out_shape=[
            jax.ShapeDtypeStruct((taps, width), F32),
            jax.ShapeDtypeStruct((1, width), F32),
            jax.ShapeDtypeStruct((ROWS + 1, words, SPAN), F32),
        ],
        scratch_shapes=[
            pltpu.VMEM((2 * SPAN, STEPS * width), BF16),
            pltpu.VMEM((words, STEPS * width), BF16),
            pltpu.VMEM((2 * SPAN, STEPS * width), F32),
        ],
        compiler_params=pltpu.CompilerParams(vmem_limit_bytes=VMEM_LIMIT),
        cost_estimate=FREE,
    )(*operands)


def table_kernel(ids_ref, embed_grad, table_out, hot):
    vocab, words = hot.shape[0], ids_ref.shape[1]
    high = embed_grad[:ROWS].reshape(ROWS * words, SPAN) * 2.0
    low = high.astype(BF16)
    pair = jnp.concatenate([low, (high - low.astype(F32)).astype(BF16)], axis=1)
    which = lax.broadcasted_iota(jnp.int32, (vocab, words), 0)
    lane = lax.broadcasted_iota(jnp.int32, (vocab, SPAN), 1) // CHAR_DIM
    table = jnp.zeros((vocab, SPAN), F32)
    for r in range(STEPS):
        for q in range(ROWS):
            j = q * STEPS + r
            cols = slice(q * words, (q + 1) * words)
            if j < CHARS:
                hot[:, cols] = jnp.where(ids_ref[j : j + 1, :] == which, 1.0, 0.0).astype(BF16)
            else:
                hot[:, cols] = jnp.zeros((vocab, words), BF16)
        both = jnp.dot(hot[...], pair, preferred_element_type=F32)
        table = jnp.where(lane == r, both[:, :SPAN] + both[:, SPAN:], table)
    step = table_out.shape[0]
    for shift in (64, 32, 16):
        table = table + pltpu.roll(table, shift, 1)
    table_out[...] = jnp.zeros_like(table_out)
    for g in range(-(-vocab // step)):
        rows = min(step, vocab - g * step)
        cols = slice(g * CHAR_DIM, (g + 1) * CHAR_DIM)
        table_out[:rows, cols] = table[g * step : g * step + rows, cols]


def table_gradient(ids_columns, embed_grad, vocab):
    words = ids_columns.shape[1]
    rows = -(-vocab // 16) * 16
    vm = pl.BlockSpec(memory_space=pltpu.VMEM)
    return pl.pallas_call(
        table_kernel,
        in_specs=[vm, vm],
        out_specs=vm,
        out_shape=jax.ShapeDtypeStruct((-(-vocab // 64) * 8, SPAN), F32),
        scratch_shapes=[pltpu.VMEM((rows, ROWS * words), BF16)],
        compiler_params=pltpu.CompilerParams(vmem_limit_bytes=VMEM_LIMIT),
        cost_estimate=FREE,
    )(ids_columns, embed_grad)


def level_call(kernel, places, level, picks, weights, arrays, shapes, hidden=False):
    width = weights.shape[3]
    rows = arrays[0].shape[0]
    tile = rows // TILES
    weights = pltpu.with_memory_space_constraint(weights, pltpu.HBM)

    def picked(pick):
        return pl.BlockSpec((1, 2, width, width), lambda i, spots: (level, 0, spots[pick], 0))

    def tiled(shape):
        if shape[0] == rows:
            return pl.BlockSpec((tile, shape[1]), lambda i, spots: (i, 0))
        return pl.BlockSpec(shape, lambda i, spots: (0, 0))

    cost = FREE
    if hidden:
        cost = pl.CostEstimate(
            flops=8 * rows * width * width, bytes_accessed=16 * rows * width, transcendentals=0
        )
    return pl.pallas_call(
        kernel,
        grid_spec=pltpu.PrefetchScalarGridSpec(
            num_scalar_prefetch=1,
            grid=(TILES,),
            in_specs=[picked(pick) for pick in picks] + [tiled(item.shape) for item in arrays],
            out_specs=[tiled(item.shape) for item in shapes],
        ),
        out_shape=shapes,
        compiler_params=pltpu.CompilerParams(vmem_limit_bytes=VMEM_LIMIT),
        cost_estimate=cost,
    )(places, *[weights] * len(picks), *arrays)


def level_kernel(
    places, own_w, near_w, mid_w, far_w, own, near, mid, far, carried, bias,
    transform_out, gate_out, carried_out, low_out, *peers_out,
):
    if peers_out:
        ours, theirs = peers_out
        size = own.shape[1] * 4 // (places.shape[0] - 4)
        count = own.shape[1] // size
        for r, piece in enumerate((own, near, mid, far)):
            for h in range(count):
                spot = places[4 + places[r] * count + h]
                half = (places.shape[0] - 4) // 2
                block = piece[:, h * size : (h + 1) * size]

                @pl.when(spot < half)
                def _():
                    ours[:, pl.ds(pl.multiple_of(spot * size, size), size)] = block

                @pl.when(spot >= half)
                def _():
                    theirs[:, pl.ds(pl.multiple_of((spot - half) * size, size), size)] = block

    parts = []
    for j in range(2):
        total = dot(own[...], own_w[0, j]) + dot(near[...], near_w[0, j])
        total = total + dot(mid[...], mid_w[0, j]) + dot(far[...], far_w[0, j])
        parts.append(total + bias[j : j + 1, :])
    transform, gate = parts
    transform_out[...] = transform
    gate_out[...] = gate
    opened = 1.0 / (1.0 + jnp.exp(-gate))
    swished = transform / (1.0 + jnp.exp(-transform))
    mixed = opened * swished + (1.0 - opened) * carried[...].astype(F32)
    carried_out[...] = mixed
    low_out[...] = mixed.astype(BF16)


def level_back_kernel(places, far_w, mid_w, transform, gate, carried, grad, both_out, carry_out, bias_out, far_out, mid_out):
    width = transform.shape[1]
    value = grad[...]
    opened = 1.0 / (1.0 + jnp.exp(-gate[...]))
    squashed = 1.0 / (1.0 + jnp.exp(-transform[...]))
    swished = transform[...] * squashed
    slope = value * opened
    first = slope * (squashed * (1.0 + transform[...] * (1.0 - squashed)))
    second = (slope * (1.0 - opened)) * (swished - carried[...].astype(F32))
    carry_out[...] = value - slope
    both_out[:, :width] = first.astype(BF16)
    both_out[:, width:] = second.astype(BF16)

    @pl.when(pl.program_id(0) == 0)
    def _():
        bias_out[...] = jnp.zeros_like(bias_out)

    bias_out[:, :width] += jnp.sum(first.astype(BF16).astype(F32), axis=0, keepdims=True)
    bias_out[:, width:] += jnp.sum(second.astype(BF16).astype(F32), axis=0, keepdims=True)
    far_out[...] = back_product(both_out, far_w).astype(BF16)
    mid_out[...] = back_product(both_out, mid_w)


def back_product(both, weights):
    width = weights.shape[3]
    dims = (((1,), (1,)), ((), ()))
    first = lax.dot_general(both[:, :width], weights[0, 0], dims, preferred_element_type=F32)
    return first + lax.dot_general(both[:, width:], weights[0, 1], dims, preferred_element_type=F32)


def level_rest_kernel(places, near_w, own_w, both, carry, near_out, own_out):
    near_out[...] = back_product(both, near_w).astype(BF16)
    own_out[...] = back_product(both, own_w) + carry[...]


NT = (((1,), (1,)), ((), ()))
TN = (((0,), (0,)), ((), ()))


def dot(left, right, dims=(((1,), (0,)), ((), ()))):
    return lax.dot_general(left, right, dims, preferred_element_type=F32)


def local_call(kernel, arrays, shapes, scalars=None, cost=FREE):
    vm = pl.BlockSpec(memory_space=pltpu.VMEM)
    specs = [vm] * len(arrays)
    if scalars is not None:
        arrays = (scalars, *arrays)
        specs = [pl.BlockSpec(memory_space=pltpu.SMEM)] + specs
    return pl.pallas_call(
        kernel,
        in_specs=specs,
        out_specs=[vm] * len(shapes),
        out_shape=[jax.ShapeDtypeStruct(shape, kind) for shape, kind in shapes],
        compiler_params=pltpu.CompilerParams(vmem_limit_bytes=VMEM_LIMIT),
        cost_estimate=cost,
    )(*arrays)


def center_scale(total):
    center = total - jnp.mean(total, axis=-1, keepdims=True)
    return center, lax.rsqrt(jnp.mean(center * center, axis=-1, keepdims=True) + EPSILON)


def norm_kernel(pair, got, bias, base, gain, shift, total_out, hidden_out, low_out):
    total = pair[...].astype(F32) + got[...].astype(F32) + bias[...] + base[...]
    center, spread = center_scale(total)
    hidden = center * spread * gain[...] + shift[...]
    total_out[...] = total
    hidden_out[...] = hidden
    low_out[...] = hidden.astype(BF16)


def norm_back(total, gain, grad, grad_out, low_out, sums_out):
    center, spread = center_scale(total)
    normed = center * spread
    inner = grad * gain
    mean_inner = jnp.mean(inner, axis=-1, keepdims=True)
    mean_both = jnp.mean(inner * normed, axis=-1, keepdims=True)
    result = spread * (inner - mean_inner - normed * mean_both)
    low = result.astype(BF16)
    grad_out[...] = result
    low_out[...] = low
    sums_out[0:1, :] = jnp.sum(grad * normed, axis=0, keepdims=True)
    sums_out[1:2, :] = jnp.sum(grad, axis=0, keepdims=True)
    sums_out[2:3, :] = jnp.sum(low.astype(F32), axis=0, keepdims=True)


def last_norm_kernel(
    pair, got, bias, base, gain, shift, out_grad, encoded_out, grad_out, low_out, sums_out
):
    total = pair[...].astype(F32) + got[...].astype(F32) + bias[...] + base[...]
    center, spread = center_scale(total)
    encoded_out[...] = center * spread * gain[...] + shift[...]
    norm_back(total, gain[...], out_grad[...], grad_out, low_out, sums_out)


def norm_back_kernel(pair, got, base, total, gain, grad_out, low_out, sums_out):
    grad = pair[...].astype(F32) + got[...].astype(F32) + base[...]
    norm_back(total[...], gain[...], grad, grad_out, low_out, sums_out)


def project_kernel(perm, inputs, weight, own_out, send_out):
    half = own_out.shape[0]
    state = dot(perm[...], inputs[...]).astype(BF16)
    own_out[...] = state[:half]
    send_out[...] = dot(state[half:], weight[...]).astype(BF16)


def project_back_kernel(own, other, perm, weight, words_out, grad_out):
    half = own.shape[0]
    words = dot(perm[:half], own[...], TN) + dot(perm[half:], other[...], TN)
    words = words.astype(BF16)
    words_out[...] = words
    grad_out[...] = dot(words, weight[...], NT)


def head_probs(qkv, head, width, same):
    query = qkv[:, head * HEAD : (head + 1) * HEAD]
    keys = qkv[:, width + head * HEAD : width + (head + 1) * HEAD]
    scores = jnp.where(same, dot(query, keys, NT) * HEAD ** (-0.5), NEGATIVE)
    exps = jnp.exp(scores - jnp.max(scores, axis=-1, keepdims=True))
    return query, keys, exps * (1.0 / jnp.sum(exps, axis=-1, keepdims=True))


def attend_kernel(own, other, weight, biases, column, row, out_w, qkv_out, mixed_out, send_out):
    half, width = own.shape[0], out_w.shape[0]
    for rows, part in ((slice(0, half), own), (slice(half, 2 * half), other)):
        product = dot(part[...], weight[...], NT)
        qkv_out[rows, :width] = (product[:, :width] + biases[0:1, :]).astype(BF16)
        qkv_out[rows, width : 2 * width] = product[:, width : 2 * width].astype(BF16)
        qkv_out[rows, 2 * width :] = (product[:, 2 * width :] + biases[1:2, :]).astype(BF16)
    qkv = qkv_out[...]
    same = column[...] == row[...]
    for head in range(width // HEAD):
        _, _, probs = head_probs(qkv, head, width, same)
        values = qkv[:, 2 * width + head * HEAD : 2 * width + (head + 1) * HEAD]
        mixed_out[:, head * HEAD : (head + 1) * HEAD] = dot(probs.astype(BF16), values).astype(BF16)
    send_out[...] = dot(mixed_out[half:, :], out_w[...]).astype(BF16)


def attend_back_kernel(own, other, out_w, qkv_ref, column, row, weight, grad_out, sums_out, send_out):
    half, width = own.shape[0], out_w.shape[0]
    qkv = qkv_ref[...]
    same = column[...] == row[...]
    mixed = jnp.concatenate(
        [dot(part[...], out_w[...], NT).astype(BF16) for part in (own, other)], axis=0
    )
    scale = HEAD ** (-0.5)
    for head in range(width // HEAD):
        query, keys, probs = head_probs(qkv, head, width, same)
        values = qkv[:, 2 * width + head * HEAD : 2 * width + (head + 1) * HEAD]
        grads = mixed[:, head * HEAD : (head + 1) * HEAD]
        inner = dot(grads, values, NT)
        slope = probs * (inner - jnp.sum(probs * inner, axis=-1, keepdims=True))
        slope = slope.astype(BF16)
        parts = (
            dot(slope, keys) * scale,
            dot(slope, query, TN) * scale,
            dot(probs.astype(BF16), grads, TN),
        )
        for j, part in enumerate(parts):
            first = j * width + head * HEAD
            grad_out[:, first : first + HEAD] = part.astype(BF16)
    sums_out[...] = jnp.sum(grad_out[...].astype(F32), axis=0, keepdims=True)
    send_out[...] = dot(grad_out[half:, :], weight[...]).astype(BF16)


def gelu_parts(value):
    scale = 0.7978845608028654
    square = value * value
    t = jnp.tanh(scale * value * (1.0 + 0.044715 * square))
    return t, scale * (1.0 + 3 * 0.044715 * square)


def feed_kernel(own, other, up_w, up_b, down_w, upward_out, active_out, send_out):
    half = own.shape[0]
    for rows, part in ((slice(0, half), own), (slice(half, 2 * half), other)):
        upward = dot(part[...], up_w[...]) + up_b[...]
        t, _ = gelu_parts(upward)
        upward_out[rows, :] = upward
        active_out[rows, :] = (0.5 * upward * (1.0 + t)).astype(BF16)
    send_out[...] = dot(active_out[half:, :], down_w[...]).astype(BF16)


def feed_back_kernel(own, other, down_w, upward_ref, up_w, grad_out, sums_out, send_out):
    half = own.shape[0]
    total = jnp.zeros(sums_out.shape, F32)
    for rows, part in ((slice(0, half), own), (slice(half, 2 * half), other)):
        grad = dot(part[...], down_w[...], NT)
        upward = upward_ref[rows, :]
        t, inner = gelu_parts(upward)
        slope = 0.5 * (1.0 + t) + 0.5 * upward * (1.0 - t * t) * inner
        low = (grad * slope).astype(BF16)
        grad_out[rows, :] = low
        total = total + jnp.sum(low.astype(F32), axis=0, keepdims=True)
    sums_out[...] = total
    send_out[...] = dot(grad_out[half:, :], up_w[...], NT).astype(BF16)


def products_kernel(counts, spots, *refs):
    *operands, keep, send = refs
    half, rows, _ = keep.shape
    first, position = 0, 0
    for count in counts:
        lefts, right = operands[position : position + count], operands[position + count]
        position += count + 1
        width, step = right.shape[1], right.shape[0] // count
        product = sum(
            dot(left[...], right[i * step : (i + 1) * step, :], TN) for i, left in enumerate(lefts)
        )
        cols = slice(first, first + width)
        first += width
        for d in range(2 * half):
            block = product[d * rows : (d + 1) * rows].astype(BF16)

            @pl.when(spots[d] < half)
            def _():
                keep[spots[d], :, cols] = block

            @pl.when(spots[d] >= half)
            def _():
                send[spots[d] - half, :, cols] = block


def products(groups, spots):
    peers = spots.shape[0]
    total = sum(right.shape[1] for _, right in groups)
    shape = ((peers // 2, groups[0][0][0].shape[1] // peers, total), BF16)
    return local_call(
        functools.partial(products_kernel, [len(lefts) for lefts, _ in groups]),
        [item for lefts, right in groups for item in (*lefts, right)],
        [shape, shape],
        spots,
        pl.CostEstimate(flops=4 * 10**9, bytes_accessed=10**7, transcendentals=0),
    )


def join_kernel(count, *refs):
    for i in range(count):
        kept, got = refs[2 * i], refs[2 * i + 1]
        first, second = refs[2 * count + 2 * i], refs[2 * count + 2 * i + 1]
        half = first.shape[0]
        for j in range(half):
            first[j] = (kept[j].astype(F32) + got[j].astype(F32)).astype(BF16)
            second[j] = (kept[half + j].astype(F32) + got[half + j].astype(F32)).astype(BF16)


def join_blocks(*parts):
    shapes = []
    for kept, _ in parts:
        shapes += [((kept.shape[0] // 2, *kept.shape[1:]), BF16)] * 2
    joined = local_call(
        functools.partial(join_kernel, len(parts)), [item for pair in parts for item in pair], shapes
    )
    return [joined[2 * i : 2 * i + 2] for i in range(len(parts))]


def level_product_kernel(lower, ours, *refs):
    *theirs, half, peer, keep, send = refs
    middle, width = keep.shape
    cols = slice(lower, lower + width)
    product = dot(ours[...], half[:, cols], TN)
    first = 0
    for piece in theirs:
        product = product + dot(piece[...], peer[first : first + piece.shape[0], cols], TN)
        first += piece.shape[0]
    keep[...] = product[:middle].astype(BF16)
    send[...] = product[middle:].astype(BF16)


def level_product(ours, theirs, half, peer, lower, width):
    shape = ((ours.shape[1] // 2, width), BF16)
    return local_call(
        functools.partial(level_product_kernel, lower),
        (ours, *theirs, half, peer),
        [shape, shape],
        None,
        pl.CostEstimate(flops=4 * 10**9, bytes_accessed=10**7, transcendentals=0),
    )


def fence(*values):
    return lax.optimization_barrier(values)


def swap(values, axis, bit):
    count = lax.axis_size(axis)
    return lax.ppermute(values, axis, [(i, i ^ bit) for i in range(count)])


def peer_order(bits):
    count = 1 << len(bits)
    return [
        sum(bit for i, bit in enumerate(bits) if (p >> (len(bits) - 1 - i)) & 1) for p in range(count)
    ]


def blocks_by_peer(values, axis, order, count):
    size = values.shape[axis] // count
    me = lax.axis_index("dp")
    return [lax.dynamic_slice_in_dim(values, (me ^ r) * size, size, axis) for r in order]


def on_device(
    chars,
    char_mask,
    word_order,
    segment_ids,
    char_table,
    conv_weight,
    conv_bias,
    highway_weight,
    highway_bias,
    project_weight,
    project_bias,
    position_table,
    norm_gain,
    norm_bias,
    qkv_weight,
    qv_bias,
    out_weight,
    out_bias,
    up_weight,
    up_bias,
    down_weight,
    down_bias,
    out_grad,
):
    dp_count = lax.axis_size("dp")
    dp_index = lax.axis_index("dp")
    mp_index = lax.axis_index("mp")
    low = mp_index & 1
    word_count = chars.shape[0]
    per_peer = word_count // dp_count
    half_count = word_count // 2
    local_channels = conv_weight.shape[1]
    dp_bits = [1 << b for b in range(dp_count.bit_length() - 1)]
    order = peer_order(dp_bits)
    far_bits = dp_bits[1:] + dp_bits[:1]

    local_rows = (
        lax.dynamic_slice(
            word_order.reshape(dp_count, dp_count, per_peer),
            (0, dp_index, 0),
            (dp_count, 1, per_peer),
        ).reshape(word_count)
        - dp_index * word_count
    )
    places = local_rows ^ (low * half_count)
    perm = (jnp.arange(word_count, dtype=jnp.int32)[:, None] == places[None, :]).astype(BF16)

    def own_half(values):
        return lax.dynamic_slice_in_dim(values, low * half_count, half_count, 0)

    ids = jnp.where(char_mask > 0, chars, -1).reshape(dp_count, per_peer * CHARS)
    ids = lax.all_to_all(ids, "dp", split_axis=0, concat_axis=0, tiled=True)
    weights = jnp.swapaxes(highway_weight, 1, 2)
    ids, weights = fence(ids, weights)
    ids = ids.reshape(word_count, CHARS)

    used_taps = filter_mask(local_channels, mp_index * local_channels)
    filters = jnp.where(used_taps, conv_weight, jnp.zeros_like(conv_weight))
    counts = block_counts(ids, BLOCK)
    pooled, embedded = cnn_forward(
        ids, counts, spread_table(char_table), filters, conv_bias, BLOCK
    )

    def spots_of(bits):
        peers = dp_index ^ jnp.array(peer_order(bits), jnp.int32)
        index = jnp.arange(dp_count, dtype=jnp.int32)
        return jnp.sum(jnp.where(peers[None, :] == index[:, None], index[None, :], 0), axis=1)

    spots, far_spots = spots_of(dp_bits), spots_of(far_bits)
    places = jnp.concatenate([mp_index ^ jnp.arange(4, dtype=jnp.int32), spots])
    square = (word_count, local_channels)
    wide_f32 = jax.ShapeDtypeStruct(square, F32)
    wide_bf16 = jax.ShapeDtypeStruct(square, BF16)

    carried = inputs = pooled
    kept = []
    theirs = None
    for depth in range(LAYERS):
        a = inputs
        b = swap(a, "mp", 1)
        c = swap(a, "mp", 2)
        if depth:
            c, kept[0][4][0] = fence(c, kept[0][4][0])
        d = swap(c, "mp", 1)
        peer_shape = jax.ShapeDtypeStruct((word_count, CHANNELS // 2), BF16)
        direct = (CHANNELS // dp_count) % 128 == 0
        transform, gate, mixed_state, inputs, *peer_blocks = level_call(
            level_kernel,
            places,
            depth,
            (0, 1, 2, 3),
            weights,
            (a, b, c, d, carried, highway_bias[depth]),
            [wide_f32, wide_f32, wide_f32, wide_bf16] + [peer_shape] * (2 * direct),
        )
        if direct:
            ours, theirs = peer_blocks
        else:
            whole = jnp.zeros((word_count, CHANNELS), BF16)
            for r, piece in enumerate((a, b, c, d)):
                whole = lax.dynamic_update_slice(
                    whole, piece, (0, (mp_index ^ r) * local_channels)
                )
            blocks = blocks_by_peer(whole, 1, order, dp_count)
            ours = jnp.concatenate(blocks[: dp_count // 2], axis=1)
            theirs = jnp.concatenate(blocks[dp_count // 2 :], axis=1)
        step = -(-word_count // 48) * 16
        theirs = [
            swap(theirs[first : first + step], "dp", 1) for first in range(0, word_count, step)
        ]
        kept.append([carried, transform, gate, ours, theirs])
        carried = mixed_state

    width = project_weight.shape[1]
    half_f32, half_bf16 = ((half_count, width), F32), ((half_count, width), BF16)
    sums_shape = ((3, width), F32)

    def cross(own, matrix, sent, beside=None, dims=(((1,), (0,)), ((), ())), after=None):
        got = swap(sent, "mp", 1)
        pair, after = fence((dot(own, matrix, dims) + got.astype(F32)).astype(BF16), after)
        got, beside = fence(swap(pair, "mp", 2), beside)
        return (pair, got, beside) if after is None else (pair, got, beside, after)

    def row(vector):
        return vector.reshape(1, -1)

    def send(parts, bit):
        return parts[0], swap(parts[1], "dp", bit)

    def blocked(parts):
        shape = (dp_count // 4, CHANNELS // dp_count, local_channels)
        return [part.reshape(shape) for part in parts]

    def finish(parts, bits):
        for bit in bits:
            parts = send(join_blocks(parts)[0], bit)
        return parts[0][0].astype(F32) + parts[1][0].astype(F32)

    def blocked(parts):
        shape = (dp_count // 4, CHANNELS // dp_count, local_channels)
        return [part.reshape(shape) for part in parts]

    def finish(parts, bits):
        for bit in bits:
            parts = send(join_blocks(parts)[0], bit)
        return parts[0][0].astype(F32) + parts[1][0].astype(F32)

    spots = jnp.sum(
        jnp.where(
            (dp_index ^ jnp.array(order, jnp.int32))[None, :]
            == jnp.arange(dp_count, dtype=jnp.int32)[:, None],
            jnp.arange(dp_count, dtype=jnp.int32)[None, :],
            0,
        ),
        axis=1,
    )

    own_state, sent = local_call(
        project_kernel,
        (perm, inputs, project_weight),
        [((half_count, local_channels), BF16), half_bf16],
    )
    pair, got, kept[0][4][1] = cross(own_state, project_weight, sent, kept[0][4][1])
    embed_total, hidden_in, x_own = local_call(
        norm_kernel,
        (pair, got, row(project_bias), own_half(position_table), row(norm_gain[0]), row(norm_bias[0])),
        [half_f32, half_f32, half_bf16],
    )
    x_other = swap(x_own, "mp", 1)
    local_heads = qkv_weight.shape[2]
    qkv_flat = jnp.transpose(qkv_weight, (1, 2, 0)).reshape(3 * local_heads, width)
    segments = segment_ids[0]
    segments = jnp.where(low > 0, jnp.roll(segments, half_count), segments)
    column, line = segments.reshape(-1, 1), segments.reshape(1, -1)
    qkv_shape = ((word_count, 3 * local_heads), BF16)
    qkv, mixed, sent = local_call(
        attend_kernel,
        (x_own, x_other, qkv_flat, qv_bias, column, line, out_weight),
        [qkv_shape, ((word_count, local_heads), BF16), half_bf16],
    )
    pair, got, kept[0][4][2] = cross(mixed[:half_count], out_weight, sent, kept[0][4][2])
    resid_one, hidden_mid, mid_own = local_call(
        norm_kernel,
        (pair, got, row(out_bias), hidden_in, row(norm_gain[1]), row(norm_bias[1])),
        [half_f32, half_f32, half_bf16],
    )
    mid_other = swap(mid_own, "mp", 1)
    hidden_units = up_weight.shape[1]
    upward, activated, sent = local_call(
        feed_kernel,
        (mid_own, mid_other, up_weight, row(up_bias), down_weight),
        [((word_count, hidden_units), F32), ((word_count, hidden_units), BF16), half_bf16],
    )
    pair, got, kept[1][4][0] = cross(activated[:half_count], down_weight, sent, kept[1][4][0])
    encoded, resid_two_grad, down_own, sums_two = local_call(
        last_norm_kernel,
        (
            pair,
            got,
            row(down_bias),
            hidden_mid,
            row(norm_gain[2]),
            row(norm_bias[2]),
            own_half(out_grad),
        ),
        [half_f32, half_f32, half_bf16, sums_shape],
    )
    down_other = swap(down_own, "mp", 1)
    up_grad, up_bias_grad, sent = local_call(
        feed_back_kernel,
        (down_own, down_other, down_weight, upward, up_weight),
        [((word_count, hidden_units), BF16), ((1, hidden_units), F32), half_bf16],
    )
    pair, got, kept[1][4][1], up_later = cross(
        up_grad[:half_count], up_weight, sent, kept[1][4][1], NT, up_grad
    )
    resid_one_grad, attn_own, sums_one = local_call(
        norm_back_kernel,
        (pair, got, resid_two_grad, resid_one, row(norm_gain[1])),
        [half_f32, half_bf16, sums_shape],
    )
    first_blocks = products(
        [((mid_own, mid_other), up_later), ((down_own, down_other), activated)], far_spots
    )
    attn_own, first_blocks = fence(attn_own, first_blocks)
    first_parts = send(first_blocks, far_bits[0])
    attn_other = swap(attn_own, "mp", 1)
    qkv_grad, qkv_sums, sent = local_call(
        attend_back_kernel,
        (attn_own, attn_other, out_weight, qkv, column, line, qkv_flat),
        [qkv_shape, ((1, 3 * local_heads), F32), half_bf16],
    )
    pair, got, kept[1][4][2] = cross(qkv_grad[:half_count], qkv_flat, sent, kept[1][4][2])
    embed_grad, proj_own, sums_zero = local_call(
        norm_back_kernel,
        (pair, got, resid_one_grad, embed_total, row(norm_gain[0])),
        [half_f32, half_bf16, sums_shape],
    )
    proj_other = swap(proj_own, "mp", 1)
    proj_words, state_grad = local_call(
        project_back_kernel,
        (proj_own, proj_other, perm, project_weight),
        [((word_count, width), BF16), ((word_count, local_channels), F32)],
    )
    def level_back(depth, grad, before, beside, after):
        carried_now, transform_now, gate_now, _, _ = kept[depth]
        both_low, carry, bias_sum, far, mid = level_call(
            level_back_kernel,
            places,
            depth,
            (3, 2),
            weights,
            (transform_now, gate_now, carried_now, grad),
            [
                jax.ShapeDtypeStruct((word_count, 2 * local_channels), BF16),
                wide_f32,
                jax.ShapeDtypeStruct((1, 2 * local_channels), F32),
                wide_bf16,
                wide_f32,
            ],
        )
        got = swap(far, "mp", 1)
        pair = (mid + got.astype(F32)).astype(BF16)
        pair, later, before, after = fence(pair, both_low, before, after)
        near, own = level_call(
            level_rest_kernel, places, depth, (1, 0), weights, (later, carry), [wide_bf16, wide_f32]
        )
        halves = [both_low]
        if not depth:
            halves = [both_low[:, :local_channels], both_low[:, local_channels:]]
        peers = [swap(half, "dp", 1) for half in halves]
        crossing, peers[0], beside = fence(swap(pair, "mp", 2), peers[0], beside)
        below = own + swap(near, "mp", 1).astype(F32) + crossing.astype(F32)
        return below, bias_sum.reshape(2, local_channels), halves, peers, before, beside, after

    def level_part(depth, half, peer, column=0):
        return level_product(
            kept[depth][3], kept[depth][4], half, peer, column * local_channels, local_channels
        )

    def exchange(values, bit):
        sent = fence(values.astype(BF16))[0]
        return sent, swap(sent, "dp", bit)

    def combine(parts):
        return parts[0].astype(F32) + parts[1].astype(F32)

    def complete(parts, bits):
        for bit in bits:
            parts = exchange(combine(parts), bit)
        return combine(parts)

    def rows_of(values, rows):
        values = values.reshape(-1, values.shape[-1])
        return jnp.pad(values, ((0, rows - values.shape[0]), (0, width - values.shape[1])))

    row_pack = jnp.concatenate([sums_zero, sums_one, sums_two], axis=0)
    row_pack = row_pack + swap(row_pack, "mp", 1)
    quarter = half_count // 2
    high = (mp_index >> 1) & 1
    position_part = lax.dynamic_slice_in_dim(embed_grad, high * quarter, quarter, 0)
    small_rows = -(-(row_pack.shape[0] + 2) // 16) * 16
    small_pack = jnp.concatenate(
        [row_pack, rows_of(up_bias_grad, 1), rows_of(qkv_sums, small_rows - row_pack.shape[0] - 1)],
        axis=0,
    )

    state_grad, bias_one, halves_one, peers_one, _, first_parts, words_later = level_back(
        1, state_grad, None, first_parts, proj_words
    )
    first_parts = send(join_blocks(first_parts)[0], far_bits[1])
    second_blocks = products(
        [((x_own, x_other), qkv_grad), ((attn_own, attn_other), mixed), ((words_later,), inputs)],
        spots,
    )
    early = jnp.concatenate([position_part, small_pack], axis=0).astype(BF16)
    state_grad, second_blocks, early = fence(state_grad, second_blocks, early)
    early = exchange(early, dp_bits[0])
    first_one = level_part(1, halves_one[0], peers_one[0], 0)
    state_grad, bias_zero, halves_zero, peers_zero, first_one, beside, later = level_back(
        0, state_grad, first_one, (first_parts, early), (halves_one[0], peers_one[0])
    )
    first_parts, early = beside
    first_one = send(blocked(first_one), dp_bits[1])
    second_one = level_part(1, *later, 1)
    state_grad, second_one = fence(state_grad, second_one)
    first_zero = level_part(0, halves_zero[0], peers_zero[0])
    pooled_grad, first_zero, first_one, second_blocks = fence(
        state_grad.astype(BF16), first_zero, first_one, second_blocks
    )
    first_parts = join_blocks(first_parts)[0]
    first_one = send(join_blocks(first_one)[0], dp_bits[2])
    second_parts = send(second_blocks, dp_bits[0])
    second_one = send(blocked(second_one), dp_bits[1])
    first_zero = send(blocked(first_zero), dp_bits[1])

    middle = local_channels // 2
    lower, upper = slice(0, middle), slice(middle, local_channels)
    cnn_out = cnn_backward(
        counts, embedded, filters[:, lower], conv_bias[lower], pooled_grad[:, lower], None, BLOCK
    )
    (conv_low, bias_low, embed_part), first_one, second_one, first_zero, peers_zero[1] = fence(
        cnn_out, first_one, second_one, first_zero, peers_zero[1]
    )
    second_zero = level_part(0, halves_zero[1], peers_zero[1])
    second_one, first_zero = join_blocks(second_one, first_zero)
    second_parts = join_blocks(second_parts)[0]
    embed_part, second_one, first_zero, second_zero, second_parts, early = fence(
        embed_part, second_one, first_zero, second_zero, second_parts, combine(early)
    )
    second_zero = send(blocked(second_zero), dp_bits[1])
    second_one = send(second_one, dp_bits[2])
    first_zero = send(first_zero, dp_bits[2])
    second_parts = send(second_parts, dp_bits[1])
    early = exchange(early, dp_bits[1])
    cnn_out = cnn_backward(
        counts, embedded, filters[:, upper], conv_bias[upper], pooled_grad[:, upper], embed_part, BLOCK
    )
    (conv_high, bias_high, embed_part), second_one, first_zero, second_zero, early, first_parts = fence(
        cnn_out, second_one, first_zero, second_zero, early, first_parts
    )
    second_zero = send(join_blocks(second_zero)[0], dp_bits[2])
    early = exchange(combine(early), dp_bits[2])
    first_sum = finish(send(first_parts, far_bits[2]), far_bits[3:])
    conv_sum = jnp.concatenate([conv_low, conv_high], axis=1)
    conv_pack = jnp.concatenate(
        [
            jnp.where(used_taps, conv_sum, jnp.zeros_like(conv_sum)),
            jnp.concatenate([bias_low, bias_high], axis=1),
            bias_zero,
            bias_one,
        ],
        axis=0,
    )
    conv_rows = conv_sum.shape[0]
    conv_pack = jnp.pad(conv_pack, ((0, -conv_pack.shape[0] % 16), (0, 0)))
    conv_parts = exchange(conv_pack, dp_bits[0])
    table_sum = table_gradient(ids.T, embed_part, char_table.shape[0])
    table_sum, conv_parts, second_parts = fence(table_sum, conv_parts, second_parts)
    second_parts = send(join_blocks(second_parts)[0], dp_bits[2])
    conv_parts = exchange(combine(conv_parts), dp_bits[1])
    table_total = table_sum
    table_total = table_total + swap(table_total, "mp", 1)
    table_total = table_total + swap(table_total, "mp", 2)
    table_total, conv_parts = fence(table_total, conv_parts)
    conv_parts = exchange(combine(conv_parts), dp_bits[2])
    for bit in dp_bits:
        table_total = table_total + swap(table_total, "dp", bit)
    table_total = table_total.reshape(-1, STEPS, CHAR_DIM)
    table_total = jnp.swapaxes(table_total, 0, 1).reshape(-1, CHAR_DIM)[: char_table.shape[0]]
    conv_pack = complete(conv_parts, dp_bits[3:])
    conv_sums = (
        conv_pack[:conv_rows],
        conv_pack[conv_rows],
        conv_pack[conv_rows + 1 : conv_rows + 5].reshape(LAYERS, 2, local_channels),
    )
    second_sum = finish(second_parts, dp_bits[3:])
    level_sums = [
        jnp.stack([finish(parts, dp_bits[3:]) for parts in level], axis=1)
        for level in ((first_zero, second_zero), (first_one, second_one))
    ]
    highway_weight_grad = jnp.stack(level_sums, axis=0)
    early = complete(early, dp_bits[3:])
    position_part, small_pack = early[:quarter], early[quarter:]
    rows = row_pack.shape[0]
    sums_zero, sums_one, sums_two = (small_pack[3 * i : 3 * i + 3] for i in range(3))
    up_bias_grad = small_pack[rows : rows + 1]
    qkv_sums = small_pack[rows + 1 : rows + 2, : 3 * local_heads]
    qv_bias_grad = jnp.stack(
        [qkv_sums[0, :local_heads], qkv_sums[0, 2 * local_heads :]], axis=0
    )
    position_part = fence(position_part.astype(BF16))[0]
    position_other = swap(position_part, "mp", 2)
    position_half = jnp.concatenate(
        [
            jnp.where(high > 0, position_other, position_part),
            jnp.where(high > 0, position_part, position_other),
        ],
        axis=0,
    )

    def both_halves(values):
        return jnp.concatenate([values, swap(values, "mp", 1)], axis=0)

    position_grad = both_halves(position_half).astype(F32)

    def in_order(values):
        first, second = values[:half_count], values[half_count:]
        return jnp.concatenate(
            [jnp.where(low > 0, second, first), jnp.where(low > 0, first, second)], axis=0
        )

    def split(total, widths):
        parts, first = [], 0
        for width in widths:
            parts.append(total[:, first : first + width])
            first += width
        return parts

    up_sum, down_sum = split(first_sum, (up_weight.shape[1], down_weight.shape[0]))
    qkv_sum, out_sum, project_sum = split(
        second_sum, (3 * local_heads, local_heads, local_channels)
    )
    return (
        in_order(both_halves(encoded)),
        table_total,
        conv_sums[0],
        conv_sums[1],
        highway_weight_grad,
        conv_sums[2],
        project_sum.T,
        sums_zero[2],
        in_order(position_grad),
        jnp.stack([sums_zero[0], sums_one[0], sums_two[0]], axis=0),
        jnp.stack([sums_zero[1], sums_one[1], sums_two[1]], axis=0),
        qkv_sum.reshape(-1, 3, local_heads),
        qv_bias_grad,
        out_sum.T,
        sums_one[2],
        up_sum,
        up_bias_grad[0],
        down_sum.T,
        sums_two[2],
    )


def solution(mesh):
    return jax.shard_map(
        on_device,
        mesh=mesh,
        in_specs=(
            P("dp", None),
            P("dp", None),
            P(),
            P("dp", None),
            P(),
            P(None, "mp"),
            P("mp"),
            P(None, None, None, "mp"),
            P(None, None, "mp"),
            P("mp", None),
            P(),
            P(),
            P(),
            P(),
            P(None, None, "mp"),
            P(None, "mp"),
            P("mp", None),
            P(),
            P(None, "mp"),
            P("mp"),
            P("mp", None),
            P(),
            P("dp", None),
        ),
        out_specs=(
            P("dp", None),
            P(),
            P(None, "mp"),
            P("mp"),
            P(None, "dp", None, "mp"),
            P(None, None, "mp"),
            P("mp", "dp"),
            P(),
            P(),
            P(),
            P(),
            P("dp", None, "mp"),
            P(None, "mp"),
            P("mp", "dp"),
            P(),
            P("dp", "mp"),
            P("mp"),
            P("mp", "dp"),
            P(),
        ),
        check_vma=False,
    )
```

profile of v0, /device:TPU:1, one launch (start us, length us, event | category | flops | bytes accessed | tf_op | source)
XLA Modules:
  0.0 397.7 jit_solution(18209583580489886542)
XLA Ops:
  3.8 6.4 %all-to-all-start = ((s32[8,1,3200]{2,1,0:T(1,128)}), s32[8,1,3200]{2,1,0:T(1,128)S(1)}, u32[]{:S(2)}, u32[]{:S(2)}) async-start(s32[8,1,3200]{2,1,0:T(1,128)} %all_to_all.11), calls=%async_computation | async-start | bytes 204800 | tf_op jit(solution)/shard_map/all_to_all | solution.py:719
  11.3 8.2 %copy.128 = bf16[2,2048,2,512]{3,1,2,0:T(8,128)(2,1)} copy(bf16[2,2048,2,512]{3,2,1,0:T(2,128)(2,1)} %param.33) | data formatting | bytes 16777216 | tf_op args[7]
  25.2 19.8 %shard_map.393 = (bf16[512,512]{1,0:T(8,128)(2,1)}, bf16[8,512,128]{2,1,0:T(8,128)(2,1)S(1)}) custom-call(s32[11]{0:T(128)S(1)} %pad_add_fusion.2.counts, s32[7,512,8]{2,1,0:T(8,128)S(1)} %bitcast.78, bf16[2176,128]{1,0:T(8,128)(2,1)S(1)} %copy-done.12, bf16[112,512]{1,0:T(8,128)(2,1)S(1)} %compare_select_fusion.1.filters_ref, f32[1,512]{1,0:T(1,128)S(1)} %bitcast.87), custom_call_target="tpu_custom_call" | custom-call | flops 1 | bytes 1 | tf_op jit(solution)/shard_map/pallas_call | solution.py:113
  48.5 10.2 %collective-permute-done.1.mid = bf16[512,512]{1,0:T(8,128)(2,1)S(1)} collective-permute-done((bf16[512,512]{1,0:T(8,128)(2,1)}, bf16[512,512]{1,0:T(8,128)(2,1)S(1)}, u32[]{:S(2)}, u32[]{:S(2)}) %collective-permute-start.1) | collective-permute-done | bytes 524320 | tf_op jit(solution)/shard_map/ppermute | solution.py:651
  62.1 6.1 %shard_map.394 = (f32[512,512]{1,0:T(8,128)S(1)}, f32[512,512]{1,0:T(8,128)S(1)}, f32[512,512]{1,0:T(8,128)S(1)}, bf16[512,512]{1,0:T(8,128)(2,1)S(1)}, bf16[512...) custom-call(s32[12]{0:T(128)S(1)} %pad_add_fusion.1.places, bf16[2,2,2048,512]{3,2,1,0:T(8,128)(2,1)} %bitcast.93, ...), custom_call_target="tpu_custom_call" | custom-call | flops 1 | bytes 1 | tf_op jit(solution)/shard_map/pallas_call | solution.py:312
  75.7 6.9 %collective-permute-done.5.refs_0_ = bf16[176,1024]{1,0:T(8,128)(2,1)S(1)} collective-permute-done((bf16[176,1024]{1,0:T(8,128)(2,1)S(1)}, bf16[176,1024]{1,0:T(8,128)(2,1)S(1)}, u32[]{:S(2)}, u32[]{:S(2)}) %collective-permute-start.5) | collective-permute-done | bytes 360480 | tf_op jit(solution)/shard_map/ppermute | solution.py:651
  89.6 7.2 %shard_map.395 = (f32[512,512]{1,0:T(8,128)S(1)}, f32[512,512]{1,0:T(8,128)S(1)}, f32[512,512]{1,0:T(8,128)}, bf16[512,512]{1,0:T(8,128)(2,1)S(1)}, bf16[512,102...) custom-call(s32[12]{0:T(128)S(1)} %pad_add_fusion.1.places, bf16[2,2,2048,512]{3,2,1,0:T(8,128)(2,1)} %bitcast.97, ...), custom_call_target="tpu_custom_call" | custom-call | flops 1 | bytes 1 | tf_op jit(solution)/shard_map/pallas_call | solution.py:312
  104.1 5.2 %collective-permute-done.9.refs_1_ = bf16[176,1024]{1,0:T(8,128)(2,1)} collective-permute-done((bf16[176,1024]{1,0:T(8,128)(2,1)}, bf16[176,1024]{1,0:T(8,128)(2,1)}, u32[]{:S(2)}, u32[]{:S(2)}) %collective-permute-start.9) | collective-permute-done | bytes 360480 | tf_op jit(solution)/shard_map/ppermute | solution.py:651
  123.9 7.3 %collective-permute-done.13.refs_2_ = bf16[160,1024]{1,0:T(8,128)(2,1)S(1)} collective-permute-done((bf16[160,1024]{1,0:T(8,128)(2,1)S(1)}, bf16[160,1024]{1,0:T(8,128)(2,1)S(1)}, u32[]{:S(2)}, u32[]{:S(2)}) %collective-permute-start.13) | collective-permute-done | bytes 327712 | tf_op jit(solution)/shard_map/ppermute | solution.py:651
  141.0 8.0 %collective-permute-done.17.refs_0_ = bf16[176,1024]{1,0:T(8,128)(2,1)S(1)} collective-permute-done((bf16[176,1024]{1,0:T(8,128)(2,1)S(1)}, bf16[176,1024]{1,0:T(8,128)(2,1)S(1)}, u32[]{:S(2)}, u32[]{:S(2)}) %collective-permute-start.17) | collective-permute-done | bytes 360480 | tf_op jit(solution)/shard_map/ppermute | solution.py:651
  162.5 5.0 %collective-permute-done.22.refs_1_ = bf16[176,1024]{1,0:T(8,128)(2,1)S(1)} collective-permute-done((bf16[176,1024]{1,0:T(8,128)(2,1)S(1)}, bf16[176,1024]{1,0:T(8,128)(2,1)S(1)}, u32[]{:S(2)}, u32[]{:S(2)}) %collective-permute-start.22) | collective-permute-done | bytes 360480 | tf_op jit(solution)/shard_map/ppermute | solution.py:651
  171.2 4.1 %shard_map.405 = (bf16[512,576]{1,0:T(8,128)(2,1)S(1)}, f32[1,576]{1,0:T(1,128)S(1)}, bf16[256,768]{1,0:T(8,128)(2,1)S(1)}) custom-call(bf16[256,768]{1,0:T(8,128)(2,1)S(1)} %get-tuple-element.245.own.refs_3_, bf16[256,768]{1,0:T(8,128)(2,1)S(1)} %collective-permute-done.23.other.refs_4_, bf16[192,768]{1,0:T(8,128)(2,1)S(1)} %copy-done.11, ...), custom_call_target="tpu_custom_call" | custom-call | flops 1 | bytes 1 | tf_op jit(solution)/shard_map/pallas_call | solution.py:412
  179.5 7.4 %collective-permute-done.26.refs_2_ = bf16[160,1024]{1,0:T(8,128)(2,1)S(1)} collective-permute-done((bf16[160,1024]{1,0:T(8,128)(2,1)S(1)}, bf16[160,1024]{1,0:T(8,128)(2,1)S(1)}, u32[]{:S(2)}, u32[]{:S(2)}) %collective-permute-start.26) | collective-permute-done | bytes 327712 | tf_op jit(solution)/shard_map/ppermute | solution.py:651
  192.4 4.4 %shard_map.408 = (bf16[512,1024]{1,0:T(8,128)(2,1)S(1)}, f32[512,512]{1,0:T(8,128)S(1)}, f32[1,1024]{1,0:T(1,128)S(1)}, bf16[512,512]{1,0:T(8,128)(2,1)}, f32[512,512]{1,0:T(8,128)S(1)}) custom-call(s32[12]{0:T(128)S(1)} %pad_add_fusion.1.places, bf16[2,2,2048,512]{3,2,1,0:T(8,128)(2,1)} %bitcast.101, bf16[2,2,2048,512]{3,2,1,0:T(8,128)(2,1)} %bitcast.102, ...), custom_call_target="tpu_custom_call" | custom-call | flops 1 | bytes 1 | tf_op jit(solution)/shard_map/pallas_call | solution.py:312
  209.2 4.3 %shard_map.410 = (bf16[4,96,1280]{2,1,0:T(8,128)(2,1)S(1)}, bf16[4,96,1280]{2,1,0:T(8,128)(2,1)S(1)}) custom-call(s32[8]{0:T(128)S(1)} %select_reduce_fusion.1.spots, bf16[256,768]{1,0:T(8,128)(2,1)S(1)} %copy-done.47, bf16[256,768]{1,0:T(8,128)(2,1)S(1)} %copy-done.49, bf16[512,576]{1,0:T(8,128)(2,1)S(1)} %copy-done.71, bf16[256,768]{1,0:T(8,128)(2,1)S(1)} %copy-done.43, ...), custom_call_target="tpu_custom_call" | custom-call | flops 4000000000 | bytes 10000000 | tf_op jit(solution)/shard_map/pallas_call | solution.py:412
  213.5 12.9 %collective-permute-done.32.refs_1_ = bf16[4,96,1536]{2,1,0:T(8,128)(2,1)S(1)} collective-permute-done((bf16[4,96,1536]{2,1,0:T(8,128)(2,1)}, bf16[4,96,1536]{2,1,0:T(8,128)(2,1)S(1)}, u32[]{:S(2)}, u32[]{:S(2)}) %collective-permute-start.32) | collective-permute-done | bytes 1179680 | tf_op jit(solution)/shard_map/ppermute | solution.py:651
  248.1 15.7 %collective-permute-done.38.refs_1_ = bf16[2,96,1536]{2,1,0:T(8,128)(2,1)S(1)} collective-permute-done((bf16[2,96,1536]{2,1,0:T(8,128)(2,1)S(1)}, bf16[2,96,1536]{2,1,0:T(8,128)(2,1)S(1)}, u32[]{:S(2)}, u32[]{:S(2)}) %collective-permute-start.38) | collective-permute-done | bytes 589856 | tf_op jit(solution)/shard_map/ppermute | solution.py:651
  267.2 8.9 %collective-permute-done.40.refs_1_ = bf16[2,256,512]{2,1,0:T(8,128)(2,1)S(1)} collective-permute-done((bf16[2,256,512]{2,1,0:T(8,128)(2,1)S(1)}, bf16[2,256,512]{2,1,0:T(8,128)(2,1)S(1)}, u32[]{:S(2)}, u32[]{:S(2)}) %collective-permute-start.40) | collective-permute-done | bytes 524320 | tf_op jit(solution)/shard_map/ppermute | solution.py:651
  281.6 18.5 %shard_map.417 = (f32[112,256]{1,0:T(8,128)S(1)}, f32[1,256]{1,0:T(1,128)S(1)}, f32[8,512,128]{2,1,0:T(8,128)S(1)}) custom-call(s32[11]{0:T(128)S(1)} %pad_add_fusion.2.counts, bf16[8,512,128]{2,1,0:T(8,128)(2,1)S(1)} %copy-done.9, bf16[112,256]{1,0:T(8,128)(2,1)S(1)} %get-tuple-element.518.filters, f32[1,256]{1,0:T(1,128)S(1)} %bitcast.89, ...), custom_call_target="tpu_custom_call" | custom-call | flops 1 | bytes 1 | tf_op jit(solution)/shard_map/pallas_call | solution.py:231
  309.2 4.3 %collective-permute-start.48 = (bf16[2,256,512]{2,1,0:T(8,128)(2,1)}, bf16[2,256,512]{2,1,0:T(8,128)(2,1)}, u32[]{:S(2)}, u32[]{:S(2)}) collective-permute-start(bf16[2,256,512]{2,1,0:T(8,128)(2,1)} %bitcast.23), channel_id=1, source_target_pairs={{0,8},{4,12},{8,0},{12,4},{16,24},{20,28},{24,16},{28,20},{1,9},{5... | collective-permute-start | bytes 1572872 | tf_op jit(solution)/shard_map/ppermute | solution.py:651
  322.3 18.6 %shard_map.422 = (f32[112,256]{1,0:T(8,128)S(1)}, f32[1,256]{1,0:T(1,128)S(1)}, f32[8,512,128]{2,1,0:T(8,128)S(1)}) custom-call(s32[11]{0:T(128)S(1)} %pad_add_fusion.2.counts, bf16[8,512,128]{2,1,0:T(8,128)(2,1)S(1)} %copy-done.9, bf16[112,256]{1,0:T(8,128)(2,1)S(1)} %copy-done.55, f32[1,256]{1,0:T(1,128)S(1)} %bitcast.88, ...), custom_call_target="tpu_custom_call" | custom-call | flops 1 | bytes 1 | tf_op jit(solution)/shard_map/pallas_call | solution.py:231
  347.6 4.4 %shard_map.424 = f32[40,128]{1,0:T(8,128)S(1)} custom-call(s32[50,512]{1,0:T(8,128)S(1)} %bitcast.82, f32[8,512,128]{2,1,0:T(8,128)S(1)} %get-tuple-element.358.embed_grad), custom_call_target="tpu_custom_call" | custom-call | flops 1 | bytes 1 | tf_op jit(solution)/shard_map/pallas_call | solution.py:282
  352.0 6.4 %collective-permute-done.51.refs_1_ = bf16[2,96,1280]{2,1,0:T(8,128)(2,1)S(1)} collective-permute-done((bf16[2,96,1280]{2,1,0:T(8,128)(2,1)S(1)}, bf16[2,96,1280]{2,1,0:T(8,128)(2,1)S(1)}, u32[]{:S(2)}, u32[]{:S(2)}) %collective-permute-start.51) | collective-permute-done | bytes 491552 | tf_op jit(solution)/shard_map/ppermute | solution.py:651
  376.9 7.6 %collective-permute-done.56 = f32[40,128]{1,0:T(8,128)S(1)} collective-permute-done((f32[40,128]{1,0:T(8,128)S(1)}, f32[40,128]{1,0:T(8,128)S(1)}, u32[]{:S(2)}, u32[]{:S(2)}) %collective-permute-start.56) | collective-permute-done | bytes 20512 | tf_op jit(solution)/shard_map/ppermute | solution.py:651
  (487 shorter events, 187.2 us)
Async XLA Ops:
  198.8 27.6 %collective-permute-start.32 = (bf16[4,96,1536]{2,1,0:T(8,128)(2,1)}, bf16[4,96,1536]{2,1,0:T(8,128)(2,1)S(1)}, u32[]{:S(2)}, u32[]{:S(2)}) collective-permute-start(bf16[4,96,1536]{2,1,0:T(8,128)(2,1)} %copy-done.63), channel_id=1, source_target_pairs={{0,8},{4,12},{8,0},{12,4},{16,24},{20,28},{24,16},{28,20},{1,9},{5... | collective-permute-start | bytes 3538952 | tf_op jit(solution)/shard_map/ppermute | solution.py:651
  200.6 25.9 %collective-permute-start.31 = (bf16[512,1024]{1,0:T(8,128)(2,1)S(1)}, bf16[512,1024]{1,0:T(8,128)(2,1)S(1)}, u32[]{:S(2)}, u32[]{:S(2)}) collective-permute-start(bf16[512,1024]{1,0:T(8,128)(2,1)S(1)} %get-tuple-element.297.both.refs_3_), channel_id=1, source_target_pairs={{0,4},{4,0},{8,12},{12,8},{16,20},{20,16},{24,28},{28,24},{1,5},{5... | collective-permute-start | bytes 3145736 | tf_op jit(solution)/shard_map/ppermute | solution.py:651
  207.8 18.7 %collective-permute-start.29 = (bf16[512,512]{1,0:T(8,128)(2,1)S(1)}, bf16[512,512]{1,0:T(8,128)(2,1)S(1)}, u32[]{:S(2)}, u32[]{:S(2)}) collective-permute-start(bf16[512,512]{1,0:T(8,128)(2,1)S(1)} %get-tuple-element.261), channel_id=1, source_target_pairs={{0,1},{1,0},{2,3},{3,2},{4,5},{5,4},{6,7},{7,6},{8,9},{9,8},{10,11... | collective-permute-start | bytes 1572872 | tf_op jit(solution)/shard_map/ppermute | solution.py:651
  208.2 18.2 %collective-permute-start.30 = (bf16[512,512]{1,0:T(8,128)(2,1)S(1)}, bf16[512,512]{1,0:T(8,128)(2,1)S(1)}, u32[]{:S(2)}, u32[]{:S(2)}) collective-permute-start(bf16[512,512]{1,0:T(8,128)(2,1)S(1)} %add_convert_fusion.1), channel_id=1, source_target_pairs={{0,2},{1,3},{2,0},{3,1},{4,6},{5,7},{6,4},{7,5},{8,10},{9,11},{10,... | collective-permute-start | bytes 1572872 | tf_op jit(solution)/shard_map/ppermute | solution.py:651
  235.6 28.2 %collective-permute-start.38 = (bf16[2,96,1536]{2,1,0:T(8,128)(2,1)S(1)}, bf16[2,96,1536]{2,1,0:T(8,128)(2,1)S(1)}, u32[]{:S(2)}, u32[]{:S(2)}) collective-permute-start(bf16[2,96,1536]{2,1,0:T(8,128)(2,1)S(1)} %get-tuple-element.294), channel_id=1, source_target_pairs={{0,16},{4,20},{8,24},{12,28},{16,0},{20,4},{24,8},{28,12},{1,17},{... | collective-permute-start | bytes 1769480 | tf_op jit(solution)/shard_map/ppermute | solution.py:651
  242.6 21.8 %collective-permute-start.35 = (bf16[512,512]{1,0:T(8,128)(2,1)S(1)}, bf16[512,512]{1,0:T(8,128)(2,1)S(1)}, u32[]{:S(2)}, u32[]{:S(2)}) collective-permute-start(bf16[512,512]{1,0:T(8,128)(2,1)S(1)} %get-tuple-element.289), channel_id=1, source_target_pairs={{0,1},{1,0},{2,3},{3,2},{4,5},{5,4},{6,7},{7,6},{8,9},{9,8},{10,11... | collective-permute-start | bytes 1572872 | tf_op jit(solution)/shard_map/ppermute | solution.py:651
  243.2 21.1 %collective-permute-start.36 = (bf16[512,512]{1,0:T(8,128)(2,1)S(1)}, bf16[512,512]{1,0:T(8,128)(2,1)S(1)}, u32[]{:S(2)}, u32[]{:S(2)}) collective-permute-start(bf16[512,512]{1,0:T(8,128)(2,1)S(1)} %add_convert_fusion), channel_id=1, source_target_pairs={{0,2},{1,3},{2,0},{3,1},{4,6},{5,7},{6,4},{7,5},{8,10},{9,11},{10,... | collective-permute-start | bytes 1572872 | tf_op jit(solution)/shard_map/ppermute | solution.py:651
  244.1 34.0 %collective-permute-start.18 = (f32[256,768]{1,0:T(8,128)S(1)}, f32[256,768]{1,0:T(8,128)S(1)}, u32[]{:S(2)}, u32[]{:S(2)}) collective-permute-start(f32[256,768]{1,0:T(8,128)S(1)} %copy-done.29), channel_id=1, source_target_pairs={{0,1},{1,0},{2,3},{3,2},{4,5},{5,4},{6,7},{7,6},{8,9},{9,8},{10,11... | collective-permute-start | bytes 2359304 | tf_op jit(solution)/shard_map/ppermute | solution.py:651
  247.1 53.8 %collective-permute-start.44 = (bf16[512,512]{1,0:T(8,128)(2,1)S(1)}, bf16[512,512]{1,0:T(8,128)(2,1)S(1)}, u32[]{:S(2)}, u32[]{:S(2)}) collective-permute-start(bf16[512,512]{1,0:T(8,128)(2,1)S(1)} %get-tuple-element.494.refs_3_), channel_id=1, source_target_pairs={{0,4},{4,0},{8,12},{12,8},{16,20},{20,16},{24,28},{28,24},{1,5},{5... | collective-permute-start | bytes 1572872 | tf_op jit(solution)/shard_map/ppermute | solution.py:651
  276.1 28.0 %collective-permute-start.43 = (bf16[2,256,512]{2,1,0:T(8,128)(2,1)S(1)}, bf16[2,256,512]{2,1,0:T(8,128)(2,1)S(1)}, u32[]{:S(2)}, u32[]{:S(2)}) collective-permute-start(bf16[2,256,512]{2,1,0:T(8,128)(2,1)S(1)} %bitcast.92), channel_id=1, source_target_pairs={{0,8},{4,12},{8,0},{12,4},{16,24},{20,28},{24,16},{28,20},{1,9},{5... | collective-permute-start | bytes 1572872 | tf_op jit(solution)/shard_map/ppermute | solution.py:651
  277.3 27.0 %collective-permute-start.42 = (bf16[2,256,512]{2,1,0:T(8,128)(2,1)S(1)}, bf16[2,256,512]{2,1,0:T(8,128)(2,1)S(1)}, u32[]{:S(2)}, u32[]{:S(2)}) collective-permute-start(bf16[2,256,512]{2,1,0:T(8,128)(2,1)S(1)} %bitcast.90), channel_id=1, source_target_pairs={{0,8},{4,12},{8,0},{12,4},{16,24},{20,28},{24,16},{28,20},{1,9},{5... | collective-permute-start | bytes 1572872 | tf_op jit(solution)/shard_map/ppermute | solution.py:651
  277.6 31.4 %collective-permute-start.45 = (bf16[4,96,1280]{2,1,0:T(8,128)(2,1)S(1)}, bf16[4,96,1280]{2,1,0:T(8,128)(2,1)S(1)}, u32[]{:S(2)}, u32[]{:S(2)}) collective-permute-start(bf16[4,96,1280]{2,1,0:T(8,128)(2,1)S(1)} %get-tuple-element.338), channel_id=1, source_target_pairs={{0,4},{4,0},{8,12},{12,8},{16,20},{20,16},{24,28},{28,24},{1,5},{5... | collective-permute-start | bytes 2949128 | tf_op jit(solution)/shard_map/ppermute | solution.py:651
  278.3 25.8 %collective-permute-start.41 = (bf16[1,256,512]{2,1,0:T(8,128)(2,1)S(1)}, bf16[1,256,512]{2,1,0:T(8,128)(2,1)S(1)}, u32[]{:S(2)}, u32[]{:S(2)}) collective-permute-start(bf16[1,256,512]{2,1,0:T(8,128)(2,1)S(1)} %get-tuple-element.320), channel_id=1, source_target_pairs={{0,16},{4,20},{8,24},{12,28},{16,0},{20,4},{24,8},{28,12},{1,17},{... | collective-permute-start | bytes 786440 | tf_op jit(solution)/shard_map/ppermute | solution.py:651
  309.2 31.8 %collective-permute-start.48 = (bf16[2,256,512]{2,1,0:T(8,128)(2,1)}, bf16[2,256,512]{2,1,0:T(8,128)(2,1)}, u32[]{:S(2)}, u32[]{:S(2)}) collective-permute-start(bf16[2,256,512]{2,1,0:T(8,128)(2,1)} %bitcast.23), channel_id=1, source_target_pairs={{0,8},{4,12},{8,0},{12,4},{16,24},{20,28},{24,16},{28,20},{1,9},{5... | collective-permute-start | bytes 1572872 | tf_op jit(solution)/shard_map/ppermute | solution.py:651
  314.8 26.1 %collective-permute-start.46 = (bf16[1,256,512]{2,1,0:T(8,128)(2,1)}, bf16[1,256,512]{2,1,0:T(8,128)(2,1)}, u32[]{:S(2)}, u32[]{:S(2)}) collective-permute-start(bf16[1,256,512]{2,1,0:T(8,128)(2,1)} %copy-done.85), channel_id=1, source_target_pairs={{0,16},{4,20},{8,24},{12,28},{16,0},{20,4},{24,8},{28,12},{1,17},{... | collective-permute-start | bytes 786440 | tf_op jit(solution)/shard_map/ppermute | solution.py:651
  315.7 25.2 %collective-permute-start.47 = (bf16[1,256,512]{2,1,0:T(8,128)(2,1)}, bf16[1,256,512]{2,1,0:T(8,128)(2,1)}, u32[]{:S(2)}, u32[]{:S(2)}) collective-permute-start(bf16[1,256,512]{2,1,0:T(8,128)(2,1)} %copy-done.84), channel_id=1, source_target_pairs={{0,16},{4,20},{8,24},{12,28},{16,0},{20,4},{24,8},{28,12},{1,17},{... | collective-permute-start | bytes 786440 | tf_op jit(solution)/shard_map/ppermute | solution.py:651
  319.6 21.3 %collective-permute-start.49 = (bf16[144,768]{1,0:T(8,128)(2,1)}, bf16[144,768]{1,0:T(8,128)(2,1)S(1)}, u32[]{:S(2)}, u32[]{:S(2)}) collective-permute-start(bf16[144,768]{1,0:T(8,128)(2,1)} %convert_add_fusion.3), channel_id=1, source_target_pairs={{0,8},{4,12},{8,0},{12,4},{16,24},{20,28},{24,16},{28,20},{1,9},{5... | collective-permute-start | bytes 663560 | tf_op jit(solution)/shard_map/ppermute | solution.py:651
  320.9 37.5 %collective-permute-start.51 = (bf16[2,96,1280]{2,1,0:T(8,128)(2,1)S(1)}, bf16[2,96,1280]{2,1,0:T(8,128)(2,1)S(1)}, u32[]{:S(2)}, u32[]{:S(2)}) collective-permute-start(bf16[2,96,1280]{2,1,0:T(8,128)(2,1)S(1)} %copy-done.73), channel_id=1, source_target_pairs={{0,8},{4,12},{8,0},{12,4},{16,24},{20,28},{24,16},{28,20},{1,9},{5... | collective-permute-start | bytes 1474568 | tf_op jit(solution)/shard_map/ppermute | solution.py:651
  341.8 23.2 %collective-permute-start.61 = (bf16[144,768]{1,0:T(8,128)(2,1)S(1)}, bf16[144,768]{1,0:T(8,128)(2,1)S(1)}, u32[]{:S(2)}, u32[]{:S(2)}) collective-permute-start(bf16[144,768]{1,0:T(8,128)(2,1)S(1)} %add_convert_fusion.2), channel_id=1, source_target_pairs={{0,16},{4,20},{8,24},{12,28},{16,0},{20,4},{24,8},{28,12},{1,17},{... | collective-permute-start | bytes 663560 | tf_op jit(solution)/shard_map/ppermute | solution.py:651
  341.8 35.0 %collective-permute-start.64 = (bf16[1,96,1536]{2,1,0:T(8,128)(2,1)S(1)}, bf16[1,96,1536]{2,1,0:T(8,128)(2,1)S(1)}, u32[]{:S(2)}, u32[]{:S(2)}) collective-permute-start(bf16[1,96,1536]{2,1,0:T(8,128)(2,1)S(1)} %get-tuple-element.390), channel_id=1, source_target_pairs={{0,4},{4,0},{8,12},{12,8},{16,20},{20,16},{24,28},{28,24},{1,5},{5... | collective-permute-start | bytes 884744 | tf_op jit(solution)/shard_map/ppermute | solution.py:651
  344.0 26.2 %collective-permute-start.59 = (bf16[1,256,512]{2,1,0:T(8,128)(2,1)S(1)}, bf16[1,256,512]{2,1,0:T(8,128)(2,1)S(1)}, u32[]{:S(2)}, u32[]{:S(2)}) collective-permute-start(bf16[1,256,512]{2,1,0:T(8,128)(2,1)S(1)} %get-tuple-element.378), channel_id=1, source_target_pairs={{0,16},{4,20},{8,24},{12,28},{16,0},{20,4},{24,8},{28,12},{1,17},{... | collective-permute-start | bytes 786440 | tf_op jit(solution)/shard_map/ppermute | solution.py:651
  364.7 24.4 %collective-permute-start.60 = (bf16[1,96,1280]{2,1,0:T(8,128)(2,1)S(1)}, bf16[1,96,1280]{2,1,0:T(8,128)(2,1)S(1)}, u32[]{:S(2)}, u32[]{:S(2)}) collective-permute-start(bf16[1,96,1280]{2,1,0:T(8,128)(2,1)S(1)} %get-tuple-element.386), channel_id=1, source_target_pairs={{0,16},{4,20},{8,24},{12,28},{16,0},{20,4},{24,8},{28,12},{1,17},{... | collective-permute-start | bytes 737288 | tf_op jit(solution)/shard_map/ppermute | solution.py:651
  365.7 25.3 %collective-permute-start.62 = (bf16[128,768]{1,0:T(8,128)(2,1)S(1)}, bf16[128,768]{1,0:T(8,128)(2,1)S(1)}, u32[]{:S(2)}, u32[]{:S(2)}) collective-permute-start(bf16[128,768]{1,0:T(8,128)(2,1)S(1)} %slice.296), channel_id=1, source_target_pairs={{0,2},{1,3},{2,0},{3,1},{4,6},{5,7},{6,4},{7,5},{8,10},{9,11},{10,... | collective-permute-start | bytes 589832 | tf_op jit(solution)/shard_map/ppermute | solution.py:651
  370.3 23.1 %collective-permute-start.58 = (bf16[128,512]{1,0:T(8,128)(2,1)S(1)}, bf16[128,512]{1,0:T(8,128)(2,1)S(1)}, u32[]{:S(2)}, u32[]{:S(2)}) collective-permute-start(bf16[128,512]{1,0:T(8,128)(2,1)S(1)} %add_convert_fusion.3), channel_id=1, source_target_pairs={{0,16},{4,20},{8,24},{12,28},{16,0},{20,4},{24,8},{28,12},{1,17},{... | collective-permute-start | bytes 393224 | tf_op jit(solution)/shard_map/ppermute | solution.py:651
  (148 other events, 1150.9 us)
where the time goes:
time: 405 us; the launch traced here: 398 us
  waiting for transfers between devices  132 us (33%)
  Pallas kernels  125 us (31%)
  starting transfers between devices  77.3 us (19%)
  local copies, waits for them, and re-layouts  47 us (12%)
  other arithmetic  12 us (3%)
    ppermute x65, waiting for transfers between devices, swap(): return lax.ppermute(values, axis, [(i, i ^ bit) for i in range(count)])  132 us
    ppermute x65, starting transfers between devices, swap(): return lax.ppermute(values, axis, [(i, i ^ bit) for i in range(count)])  70.9 us
    pallas_call x2, Pallas kernels, cnn_backward(): pl.pallas_call(kernel, in_specs=[pl.BlockSpec(memory_space=pltpu.SMEM)] +...  37.1 us
    pallas_call x24, Pallas kernels, local_call(): pl.pallas_call(kernel, in_specs=specs, out_specs=[vm] * len(shapes), out_...  34.4 us
    unnamed x222, local copies, waits for them, and re-layouts  32.3 us
    pallas_call x6, Pallas kernels, level_call(): pl.pallas_call(kernel, grid_spec=pltpu.PrefetchScalarGridSpec(num_scalar_...  28.8 us
    pallas_call x1, Pallas kernels, cnn_forward(): pl.pallas_call(functools.partial(forward_kernel, block), in_specs=[pl.Blo...  19.8 us
  transfers between devices with their start and end apart: 66, of which 34 were waited for; matrix products, arithmetic and copies ran while one was open for 9% of the time, Pallas kernels for 18%

commit v1 on v0

--- a/solution.py
+++ b/solution.py
@@ -561,7 +561,8 @@
 
 
 def products_kernel(counts, spots, *refs):
-    *operands, keep, send = refs
+    pieces = 1 + (len(refs) - sum(counts) - len(counts) - 1)
+    operands, keep, sends = refs[: -pieces], refs[-pieces], refs[1 - pieces :]
     half, rows, _ = keep.shape
     first, position = 0, 0
     for count in counts:
@@ -572,7 +573,6 @@
             dot(left[...], right[i * step : (i + 1) * step, :], TN) for i, left in enumerate(lefts)
         )
         cols = slice(first, first + width)
-        first += width
         for d in range(2 * half):
             block = product[d * rows : (d + 1) * rows].astype(BF16)
 
@@ -582,38 +582,60 @@
 
             @pl.when(spots[d] >= half)
             def _():
-                send[spots[d] - half, :, cols] = block
-
-
-def products(groups, spots):
+                start = 0
+                for send in sends:
+                    low = max(first, start)
+                    high = min(first + width, start + send.shape[2])
+                    if low < high:
+                        send[spots[d] - half, :, low - start : high - start] = block[
+                            :, low - first : high - first
+                        ]
+                    start += send.shape[2]
+
+        first += width
+
+
+def products(groups, spots, split=0):
     peers = spots.shape[0]
     total = sum(right.shape[1] for _, right in groups)
-    shape = ((peers // 2, groups[0][0][0].shape[1] // peers, total), BF16)
+    rows = groups[0][0][0].shape[1] // peers
+    widths = [split, total - split] if split else [total]
     return local_call(
         functools.partial(products_kernel, [len(lefts) for lefts, _ in groups]),
         [item for lefts, right in groups for item in (*lefts, right)],
-        [shape, shape],
+        [((peers // 2, rows, columns), BF16) for columns in (total, *widths)],
         spots,
         pl.CostEstimate(flops=4 * 10**9, bytes_accessed=10**7, transcendentals=0),
     )
 
 
-def join_kernel(count, *refs):
-    for i in range(count):
-        kept, got = refs[2 * i], refs[2 * i + 1]
-        first, second = refs[2 * count + 2 * i], refs[2 * count + 2 * i + 1]
+def join_kernel(counts, *refs):
+    outs = refs[sum(counts) :]
+    position = 0
+    for i, count in enumerate(counts):
+        kept, *got = refs[position : position + count]
+        position += count
+        first, second = outs[2 * i], outs[2 * i + 1]
         half = first.shape[0]
         for j in range(half):
-            first[j] = (kept[j].astype(F32) + got[j].astype(F32)).astype(BF16)
-            second[j] = (kept[half + j].astype(F32) + got[half + j].astype(F32)).astype(BF16)
+            start = 0
+            for piece in got:
+                cols = slice(start, start + piece.shape[2])
+                start += piece.shape[2]
+                first[j, :, cols] = (kept[j, :, cols].astype(F32) + piece[j].astype(F32)).astype(BF16)
+                second[j, :, cols] = (
+                    kept[half + j, :, cols].astype(F32) + piece[half + j].astype(F32)
+                ).astype(BF16)
 
 
 def join_blocks(*parts):
     shapes = []
-    for kept, _ in parts:
+    for kept, *_ in parts:
         shapes += [((kept.shape[0] // 2, *kept.shape[1:]), BF16)] * 2
     joined = local_call(
-        functools.partial(join_kernel, len(parts)), [item for pair in parts for item in pair], shapes
+        functools.partial(join_kernel, [len(items) for items in parts]),
+        [item for items in parts for item in items],
+        shapes,
     )
     return [joined[2 * i : 2 * i + 2] for i in range(len(parts))]
 
@@ -717,8 +739,6 @@
 
     ids = jnp.where(char_mask > 0, chars, -1).reshape(dp_count, per_peer * CHARS)
     ids = lax.all_to_all(ids, "dp", split_axis=0, concat_axis=0, tiled=True)
-    weights = jnp.swapaxes(highway_weight, 1, 2)
-    ids, weights = fence(ids, weights)
     ids = ids.reshape(word_count, CHARS)
 
     used_taps = filter_mask(local_channels, mp_index * local_channels)
@@ -727,6 +747,8 @@
     pooled, embedded = cnn_forward(
         ids, counts, spread_table(char_table), filters, conv_bias, BLOCK
     )
+
+    weights = jnp.swapaxes(fence(highway_weight, pooled)[0], 1, 2)
 
     def spots_of(bits):
         peers = dp_index ^ jnp.array(peer_order(bits), jnp.int32)
@@ -748,8 +770,12 @@
         c = swap(a, "mp", 2)
         if depth:
             c, kept[0][4][0] = fence(c, kept[0][4][0])
+        else:
+            c, weights = fence(c, weights)
         d = swap(c, "mp", 1)
         peer_shape = jax.ShapeDtypeStruct((word_count, CHANNELS // 2), BF16)
+        far_peer = pltpu.HBM(peer_shape.shape, BF16)
+        far_f32 = pltpu.HBM(square, F32)
         direct = (CHANNELS // dp_count) % 128 == 0
         transform, gate, mixed_state, inputs, *peer_blocks = level_call(
             level_kernel,
@@ -758,7 +784,7 @@
             (0, 1, 2, 3),
             weights,
             (a, b, c, d, carried, highway_bias[depth]),
-            [wide_f32, wide_f32, wide_f32, wide_bf16] + [peer_shape] * (2 * direct),
+            [far_f32, far_f32, wide_f32, wide_bf16] + [far_peer, peer_shape] * direct,
         )
         if direct:
             ours, theirs = peer_blocks
@@ -873,31 +899,37 @@
         [half_f32, half_f32, half_bf16, sums_shape],
     )
     down_other = swap(down_own, "mp", 1)
+    encoded_other = swap(encoded, "mp", 1)
     up_grad, up_bias_grad, sent = local_call(
         feed_back_kernel,
         (down_own, down_other, down_weight, upward, up_weight),
         [((word_count, hidden_units), BF16), ((1, hidden_units), F32), half_bf16],
     )
-    pair, got, kept[1][4][1], up_later = cross(
-        up_grad[:half_count], up_weight, sent, kept[1][4][1], NT, up_grad
-    )
+    pair, got, beside, up_later = cross(
+        up_grad[:half_count], up_weight, sent, (kept[1][4][1], encoded_other), NT, up_grad
+    )
+    kept[1][4][1], encoded_other = beside
     resid_one_grad, attn_own, sums_one = local_call(
         norm_back_kernel,
         (pair, got, resid_two_grad, resid_one, row(norm_gain[1])),
         [half_f32, half_bf16, sums_shape],
     )
     first_blocks = products(
-        [((mid_own, mid_other), up_later), ((down_own, down_other), activated)], far_spots
+        [((mid_own, mid_other), up_later), ((down_own, down_other), activated)], far_spots, 512
     )
     attn_own, first_blocks = fence(attn_own, first_blocks)
-    first_parts = send(first_blocks, far_bits[0])
+    first_kept, *first_sent = first_blocks
+    first_got = [swap(piece, "dp", far_bits[0]) for piece in first_sent]
     attn_other = swap(attn_own, "mp", 1)
     qkv_grad, qkv_sums, sent = local_call(
         attend_back_kernel,
         (attn_own, attn_other, out_weight, qkv, column, line, qkv_flat),
         [qkv_shape, ((1, 3 * local_heads), F32), half_bf16],
     )
-    pair, got, kept[1][4][2] = cross(qkv_grad[:half_count], qkv_flat, sent, kept[1][4][2])
+    pair, got, beside = cross(
+        qkv_grad[:half_count], qkv_flat, sent, (kept[1][4][2], first_got[0])
+    )
+    kept[1][4][2], first_got[0] = beside
     embed_grad, proj_own, sums_zero = local_call(
         norm_back_kernel,
         (pair, got, resid_one_grad, embed_total, row(norm_gain[0])),
@@ -973,9 +1005,10 @@
     )
 
     state_grad, bias_one, halves_one, peers_one, _, first_parts, words_later = level_back(
-        1, state_grad, None, first_parts, proj_words
-    )
-    first_parts = send(join_blocks(first_parts)[0], far_bits[1])
+        1, state_grad, None, first_got[1], proj_words
+    )
+    first_got[1] = first_parts
+    first_parts = send(join_blocks((first_kept, *first_got))[0], far_bits[1])
     second_blocks = products(
         [((x_own, x_other), qkv_grad), ((attn_own, attn_other), mixed), ((words_later,), inputs)],
         spots,
@@ -984,10 +1017,11 @@
     state_grad, second_blocks, early = fence(state_grad, second_blocks, early)
     early = exchange(early, dp_bits[0])
     first_one = level_part(1, halves_one[0], peers_one[0], 0)
-    state_grad, bias_zero, halves_zero, peers_zero, first_one, beside, later = level_back(
-        0, state_grad, first_one, (first_parts, early), (halves_one[0], peers_one[0])
-    )
-    first_parts, early = beside
+    state_grad, bias_zero, halves_zero, peers_zero, before, beside, later = level_back(
+        0, state_grad, (first_one, early), first_parts, (halves_one[0], peers_one[0])
+    )
+    first_one, early = before
+    first_parts = beside
     first_one = send(blocked(first_one), dp_bits[1])
     second_one = level_part(1, *later, 1)
     state_grad, second_one = fence(state_grad, second_one)
@@ -1109,7 +1143,7 @@
         second_sum, (3 * local_heads, local_heads, local_channels)
     )
     return (
-        in_order(both_halves(encoded)),
+        in_order(jnp.concatenate([encoded, encoded_other], axis=0)),
         table_total,
         conv_sums[0],
         conv_sums[1],

time: 405 us -> 392 us (0.968)
  starting transfers between devices: 77.3 us -> 66 us
    ppermute x65 -> x66, starting transfers between devices: 70.9 us -> 59.6 us  [swap(): return lax.ppermute(values, axis, [(i, i ^ bit) for i in range(count)])]
    unnamed x222 -> x212, local copies, waits for them, and re-layouts: 32.3 us -> 23.4 us
    optimization_barrier x0 -> x1, local copies, waits for them, and re-layouts: none -> 8.19 us  [fence(): return lax.optimization_barrier(values)]
    ppermute x65 -> x66, waiting for transfers between devices: 132 us -> 128 us  [swap(): return lax.ppermute(values, axis, [(i, i ^ bit) for i in range(count)])]
    all_to_all x1, waiting for transfers between devices: 0.01 us -> 4.09 us  [on_device(): ids = lax.all_to_all(ids, 'dp', split_axis=0, concat_axis=0, tiled=True)]
  transfers between devices with their start and end apart: 66 -> 67, of which waited for: 34 -> 35; matrix products, arithmetic and copies ran while one was open for 9% -> 9% of each run, Pallas kernels for 18% -> 18%
where the time goes in v1:
time: 392 us; the launch traced here: 384 us
  waiting for transfers between devices  132 us (34%)
  Pallas kernels  123 us (31%)
  starting transfers between devices  66 us (17%)
  local copies, waits for them, and re-layouts  46.3 us (12%)
  other arithmetic  12.4 us (3%)
    ppermute x66, waiting for transfers between devices, swap(): return lax.ppermute(values, axis, [(i, i ^ bit) for i in range(count)])  128 us
    ppermute x66, starting transfers between devices, swap(): return lax.ppermute(values, axis, [(i, i ^ bit) for i in range(count)])  59.6 us
    pallas_call x2, Pallas kernels, cnn_backward(): pl.pallas_call(kernel, in_specs=[pl.BlockSpec(memory_space=pltpu.SMEM)] +...  34.9 us
    pallas_call x24, Pallas kernels, local_call(): pl.pallas_call(kernel, in_specs=specs, out_specs=[vm] * len(shapes), out_...  34.5 us
    pallas_call x6, Pallas kernels, level_call(): pl.pallas_call(kernel, grid_spec=pltpu.PrefetchScalarGridSpec(num_scalar_...  30.3 us
    unnamed x212, local copies, waits for them, and re-layouts  23.4 us
    pallas_call x1, Pallas kernels, cnn_forward(): pl.pallas_call(functools.partial(forward_kernel, block), in_specs=[pl.Blo...  19.2 us
    optimization_barrier x1, local copies, waits for them, and re-layouts, fence(): return lax.optimization_barrier(values)  8.19 us
  transfers between devices with their start and end apart: 67, of which 35 were waited for; matrix products, arithmetic and copies ran while one was open for 9% of the time, Pallas kernels for 18%

profile of v1, /device:TPU:1, one launch (start us, length us, event | category | flops | bytes accessed | tf_op | source)
XLA Modules:
  0.0 384.4 jit_solution(11303546896048413171)
XLA Ops:
  3.8 6.4 %all-to-all-start = ((s32[8,1,3200]{2,1,0:T(1,128)}), s32[8,1,3200]{2,1,0:T(1,128)S(1)}, u32[]{:S(2)}, u32[]{:S(2)}) async-start(s32[8,1,3200]{2,1,0:T(1,128)} %all_to_all.8), calls=%async_computation | async-start | bytes 204800 | tf_op jit(solution)/shard_map/all_to_all | solution.py:741
  12.3 4.1 %all-to-all-done = s32[8,1,3200]{2,1,0:T(1,128)S(1)} async-done(((s32[8,1,3200]{2,1,0:T(1,128)}), s32[8,1,3200]{2,1,0:T(1,128)S(1)}, u32[]{:S(2)}, u32[]{:S(2)}) %all-to-all-start) | async-done | bytes 102432 | tf_op jit(solution)/shard_map/all_to_all | solution.py:741
  21.3 19.2 %shard_map.393 = (bf16[512,512]{1,0:T(8,128)(2,1)}, bf16[8,512,128]{2,1,0:T(8,128)(2,1)S(1)}) custom-call(s32[11]{0:T(128)S(1)} %pad_add_fusion.2.counts, s32[7,512,8]{2,1,0:T(8,128)S(1)} %bitcast.75, bf16[2176,128]{1,0:T(8,128)(2,1)S(1)} %copy-done.12, bf16[112,512]{1,0:T(8,128)(2,1)S(1)} %compare_select_fusion.1.filters_ref, f32[1,512]{1,0:T(1,128)S(1)} %bitcast.84), custom_call_target="tpu_custom_call" | custom-call | flops 1 | bytes 1 | tf_op jit(solution)/shard_map/pallas_call | solution.py:113
  45.0 8.2 %copy.126 = bf16[2,2048,2,512]{3,1,2,0:T(8,128)(2,1)} copy(bf16[2,2048,2,512]{3,2,1,0:T(2,128)(2,1)} %param.33) | data formatting | bytes 16777216 | tf_op jit(solution)/shard_map/optimization_barrier | solution.py:668
  57.5 7.3 %shard_map.394 = (f32[512,512]{1,0:T(8,128)}, f32[512,512]{1,0:T(8,128)}, f32[512,512]{1,0:T(8,128)S(1)}, bf16[512,512]{1,0:T(8,128)(2,1)S(1)}, bf16[512,1024]{1...) custom-call(s32[12]{0:T(128)S(1)} %pad_add_fusion.1.places, bf16[2,2,2048,512]{3,2,1,0:T(8,128)(2,1)} %bitcast.90, ...), custom_call_target="tpu_custom_call" | custom-call | flops 1 | bytes 1 | tf_op jit(solution)/shard_map/pallas_call | solution.py:312
  69.3 7.8 %collective-permute-done.5.refs_0_ = bf16[176,1024]{1,0:T(8,128)(2,1)S(1)} collective-permute-done((bf16[176,1024]{1,0:T(8,128)(2,1)S(1)}, bf16[176,1024]{1,0:T(8,128)(2,1)S(1)}, u32[]{:S(2)}, u32[]{:S(2)}) %collective-permute-start.5) | collective-permute-done | bytes 360480 | tf_op jit(solution)/shard_map/ppermute | solution.py:673
  84.1 7.5 %shard_map.395 = (f32[512,512]{1,0:T(8,128)}, f32[512,512]{1,0:T(8,128)}, f32[512,512]{1,0:T(8,128)}, bf16[512,512]{1,0:T(8,128)(2,1)S(1)}, bf16[512,1024]{1,0:T(8,128)(2,1)}, /*index=5*/bf16[512,1024]{1,0:T(8,128)(2,1)S(1)}) custom-call(s32[12]{0:T(128)S(1)} %pad_add_fusion.1.places, bf16[2,2,2048,512]{3,2,1,0:T(8,128)(2,1)} %bitcast.94, ...), custom_call_target="tpu_custom_call" | custom-call | flops 1 | bytes 1 | tf_op jit(solution)/shard_map/pallas_call | solution.py:312
  97.7 5.4 %collective-permute-done.9.refs_1_ = bf16[176,1024]{1,0:T(8,128)(2,1)} collective-permute-done((bf16[176,1024]{1,0:T(8,128)(2,1)}, bf16[176,1024]{1,0:T(8,128)(2,1)}, u32[]{:S(2)}, u32[]{:S(2)}) %collective-permute-start.9) | collective-permute-done | bytes 360480 | tf_op jit(solution)/shard_map/ppermute | solution.py:673
  116.9 8.0 %collective-permute-done.13.refs_2_ = bf16[160,1024]{1,0:T(8,128)(2,1)S(1)} collective-permute-done((bf16[160,1024]{1,0:T(8,128)(2,1)S(1)}, bf16[160,1024]{1,0:T(8,128)(2,1)S(1)}, u32[]{:S(2)}, u32[]{:S(2)}) %collective-permute-start.13) | collective-permute-done | bytes 327712 | tf_op jit(solution)/shard_map/ppermute | solution.py:673
  133.9 8.7 %collective-permute-done.17.refs_0_ = bf16[176,1024]{1,0:T(8,128)(2,1)S(1)} collective-permute-done((bf16[176,1024]{1,0:T(8,128)(2,1)S(1)}, bf16[176,1024]{1,0:T(8,128)(2,1)S(1)}, u32[]{:S(2)}, u32[]{:S(2)}) %collective-permute-start.17) | collective-permute-done | bytes 360480 | tf_op jit(solution)/shard_map/ppermute | solution.py:673
  156.2 5.7 %collective-permute-done.21.refs_1_ = bf16[176,1024]{1,0:T(8,128)(2,1)S(1)} collective-permute-done((bf16[176,1024]{1,0:T(8,128)(2,1)S(1)}, bf16[176,1024]{1,0:T(8,128)(2,1)S(1)}, u32[]{:S(2)}, u32[]{:S(2)}) %collective-permute-start.21) | collective-permute-done | bytes 360480 | tf_op jit(solution)/shard_map/ppermute | solution.py:673
  173.2 8.1 %collective-permute-done.26.refs_2_ = bf16[160,1024]{1,0:T(8,128)(2,1)S(1)} collective-permute-done((bf16[160,1024]{1,0:T(8,128)(2,1)S(1)}, bf16[160,1024]{1,0:T(8,128)(2,1)S(1)}, u32[]{:S(2)}, u32[]{:S(2)}) %collective-permute-start.26) | collective-permute-done | bytes 327712 | tf_op jit(solution)/shard_map/ppermute | solution.py:673
  186.8 4.5 %shard_map.408 = (bf16[512,1024]{1,0:T(8,128)(2,1)S(1)}, f32[512,512]{1,0:T(8,128)S(1)}, f32[1,1024]{1,0:T(1,128)S(1)}, bf16[512,512]{1,0:T(8,128)(2,1)}, f32[512,512]{1,0:T(8,128)S(1)}) custom-call(s32[12]{0:T(128)S(1)} %pad_add_fusion.1.places, bf16[2,2,2048,512]{3,2,1,0:T(8,128)(2,1)} %bitcast.98, bf16[2,2,2048,512]{3,2,1,0:T(8,128)(2,1)} %bitcast.99, ...), custom_call_target="tpu_custom_call" | custom-call | flops 1 | bytes 1 | tf_op jit(solution)/shard_map/pallas_call | solution.py:312
  202.2 4.3 %shard_map.410 = (bf16[4,96,1280]{2,1,0:T(8,128)(2,1)S(1)}, bf16[4,96,1280]{2,1,0:T(8,128)(2,1)S(1)}) custom-call(s32[8]{0:T(128)S(1)} %select_reduce_fusion.1.spots, bf16[256,768]{1,0:T(8,128)(2,1)S(1)} %copy-done.45, bf16[256,768]{1,0:T(8,128)(2,1)S(1)} %copy-done.47, bf16[512,576]{1,0:T(8,128)(2,1)S(1)} %copy-done.67, bf16[256,768]{1,0:T(8,128)(2,1)S(1)} %copy-done.41, ...), custom_call_target="tpu_custom_call" | custom-call | flops 4000000000 | bytes 10000000 | tf_op jit(solution)/shard_map/pallas_call | solution.py:412
  206.5 6.0 %collective-permute-done.33.refs_2_ = bf16[4,96,1024]{2,1,0:T(8,128)(2,1)S(1)} collective-permute-done((bf16[4,96,1024]{2,1,0:T(8,128)(2,1)}, bf16[4,96,1024]{2,1,0:T(8,128)(2,1)S(1)}, u32[]{:S(2)}, u32[]{:S(2)}) %collective-permute-start.33) | collective-permute-done | bytes 786464 | tf_op jit(solution)/shard_map/ppermute | solution.py:673
  212.5 6.3 %collective-permute-done.32.refs_4_ = bf16[512,1024]{1,0:T(8,128)(2,1)S(1)} collective-permute-done((bf16[512,1024]{1,0:T(8,128)(2,1)S(1)}, bf16[512,1024]{1,0:T(8,128)(2,1)S(1)}, u32[]{:S(2)}, u32[]{:S(2)}) %collective-permute-start.32) | collective-permute-done | bytes 1048608 | tf_op jit(solution)/shard_map/ppermute | solution.py:673
  242.0 13.0 %collective-permute-done.40.refs_1_ = bf16[2,96,1536]{2,1,0:T(8,128)(2,1)S(1)} collective-permute-done((bf16[2,96,1536]{2,1,0:T(8,128)(2,1)S(1)}, bf16[2,96,1536]{2,1,0:T(8,128)(2,1)S(1)}, u32[]{:S(2)}, u32[]{:S(2)}) %collective-permute-start.40) | collective-permute-done | bytes 589856 | tf_op jit(solution)/shard_map/ppermute | solution.py:673
  258.5 7.2 %collective-permute-done.41.refs_1_ = bf16[2,256,512]{2,1,0:T(8,128)(2,1)S(1)} collective-permute-done((bf16[2,256,512]{2,1,0:T(8,128)(2,1)S(1)}, bf16[2,256,512]{2,1,0:T(8,128)(2,1)S(1)}, u32[]{:S(2)}, u32[]{:S(2)}) %collective-permute-start.41) | collective-permute-done | bytes 524320 | tf_op jit(solution)/shard_map/ppermute | solution.py:673
  270.3 17.4 %shard_map.417 = (f32[112,256]{1,0:T(8,128)S(1)}, f32[1,256]{1,0:T(1,128)S(1)}, f32[8,512,128]{2,1,0:T(8,128)S(1)}) custom-call(s32[11]{0:T(128)S(1)} %pad_add_fusion.2.counts, bf16[8,512,128]{2,1,0:T(8,128)(2,1)S(1)} %copy-done.9, bf16[112,256]{1,0:T(8,128)(2,1)S(1)} %get-tuple-element.526.filters, f32[1,256]{1,0:T(1,128)S(1)} %bitcast.86, ...), custom_call_target="tpu_custom_call" | custom-call | flops 1 | bytes 1 | tf_op jit(solution)/shard_map/pallas_call | solution.py:231
  288.5 5.3 %collective-permute-done.44.refs_3_ = bf16[2,256,512]{2,1,0:T(8,128)(2,1)S(1)} collective-permute-done((bf16[2,256,512]{2,1,0:T(8,128)(2,1)S(1)}, bf16[2,256,512]{2,1,0:T(8,128)(2,1)S(1)}, u32[]{:S(2)}, u32[]{:S(2)}) %collective-permute-start.44) | collective-permute-done | bytes 524320 | tf_op jit(solution)/shard_map/ppermute | solution.py:673
  308.0 17.5 %shard_map.422 = (f32[112,256]{1,0:T(8,128)S(1)}, f32[1,256]{1,0:T(1,128)S(1)}, f32[8,512,128]{2,1,0:T(8,128)S(1)}) custom-call(s32[11]{0:T(128)S(1)} %pad_add_fusion.2.counts, bf16[8,512,128]{2,1,0:T(8,128)(2,1)S(1)} %copy-done.9, bf16[112,256]{1,0:T(8,128)(2,1)S(1)} %copy-done.53, f32[1,256]{1,0:T(1,128)S(1)} %bitcast.85, ...), custom_call_target="tpu_custom_call" | custom-call | flops 1 | bytes 1 | tf_op jit(solution)/shard_map/pallas_call | solution.py:231
  334.4 4.4 %shard_map.424 = f32[40,128]{1,0:T(8,128)S(1)} custom-call(s32[50,512]{1,0:T(8,128)S(1)} %bitcast.79, f32[8,512,128]{2,1,0:T(8,128)S(1)} %get-tuple-element.366.embed_grad), custom_call_target="tpu_custom_call" | custom-call | flops 1 | bytes 1 | tf_op jit(solution)/shard_map/pallas_call | solution.py:282
  338.8 5.8 %collective-permute-done.52.refs_1_ = bf16[2,96,1280]{2,1,0:T(8,128)(2,1)S(1)} collective-permute-done((bf16[2,96,1280]{2,1,0:T(8,128)(2,1)S(1)}, bf16[2,96,1280]{2,1,0:T(8,128)(2,1)S(1)}, u32[]{:S(2)}, u32[]{:S(2)}) %collective-permute-start.52) | collective-permute-done | bytes 491552 | tf_op jit(solution)/shard_map/ppermute | solution.py:673
  363.6 7.6 %collective-permute-done.57 = f32[40,128]{1,0:T(8,128)S(1)} collective-permute-done((f32[40,128]{1,0:T(8,128)S(1)}, f32[40,128]{1,0:T(8,128)S(1)}, u32[]{:S(2)}, u32[]{:S(2)}) %collective-permute-start.57) | collective-permute-done | bytes 20512 | tf_op jit(solution)/shard_map/ppermute | solution.py:673
  (481 shorter events, 186.4 us)
Async XLA Ops:
  193.2 19.2 %collective-permute-start.33 = (bf16[4,96,1024]{2,1,0:T(8,128)(2,1)}, bf16[4,96,1024]{2,1,0:T(8,128)(2,1)S(1)}, u32[]{:S(2)}, u32[]{:S(2)}) collective-permute-start(bf16[4,96,1024]{2,1,0:T(8,128)(2,1)} %copy-done.63), channel_id=1, source_target_pairs={{0,8},{4,12},{8,0},{12,4},{16,24},{20,28},{24,16},{28,20},{1,9},{5... | collective-permute-start | bytes 2359304 | tf_op jit(solution)/shard_map/ppermute | solution.py:673
  194.0 24.7 %collective-permute-start.32 = (bf16[512,1024]{1,0:T(8,128)(2,1)S(1)}, bf16[512,1024]{1,0:T(8,128)(2,1)S(1)}, u32[]{:S(2)}, u32[]{:S(2)}) collective-permute-start(bf16[512,1024]{1,0:T(8,128)(2,1)S(1)} %get-tuple-element.305.both.refs_3_), channel_id=1, source_target_pairs={{0,4},{4,0},{8,12},{12,8},{16,20},{20,16},{24,28},{28,24},{1,5},{5... | collective-permute-start | bytes 3145736 | tf_op jit(solution)/shard_map/ppermute | solution.py:673
  200.7 18.1 %collective-permute-start.30 = (bf16[512,512]{1,0:T(8,128)(2,1)S(1)}, bf16[512,512]{1,0:T(8,128)(2,1)S(1)}, u32[]{:S(2)}, u32[]{:S(2)}) collective-permute-start(bf16[512,512]{1,0:T(8,128)(2,1)S(1)} %get-tuple-element.269), channel_id=1, source_target_pairs={{0,1},{1,0},{2,3},{3,2},{4,5},{5,4},{6,7},{7,6},{8,9},{9,8},{10,11... | collective-permute-start | bytes 1572872 | tf_op jit(solution)/shard_map/ppermute | solution.py:673
  201.1 17.7 %collective-permute-start.31 = (bf16[512,512]{1,0:T(8,128)(2,1)S(1)}, bf16[512,512]{1,0:T(8,128)(2,1)S(1)}, u32[]{:S(2)}, u32[]{:S(2)}) collective-permute-start(bf16[512,512]{1,0:T(8,128)(2,1)S(1)} %add_convert_fusion.1), channel_id=1, source_target_pairs={{0,2},{1,3},{2,0},{3,1},{4,6},{5,7},{6,4},{7,5},{8,10},{9,11},{10,... | collective-permute-start | bytes 1572872 | tf_op jit(solution)/shard_map/ppermute | solution.py:673
  226.4 28.6 %collective-permute-start.40 = (bf16[2,96,1536]{2,1,0:T(8,128)(2,1)S(1)}, bf16[2,96,1536]{2,1,0:T(8,128)(2,1)S(1)}, u32[]{:S(2)}, u32[]{:S(2)}) collective-permute-start(bf16[2,96,1536]{2,1,0:T(8,128)(2,1)S(1)} %get-tuple-element.303), channel_id=1, source_target_pairs={{0,16},{4,20},{8,24},{12,28},{16,0},{20,4},{24,8},{28,12},{1,17},{... | collective-permute-start | bytes 1769480 | tf_op jit(solution)/shard_map/ppermute | solution.py:673
  233.5 21.5 %collective-permute-start.37 = (bf16[512,512]{1,0:T(8,128)(2,1)S(1)}, bf16[512,512]{1,0:T(8,128)(2,1)S(1)}, u32[]{:S(2)}, u32[]{:S(2)}) collective-permute-start(bf16[512,512]{1,0:T(8,128)(2,1)S(1)} %get-tuple-element.297), channel_id=1, source_target_pairs={{0,1},{1,0},{2,3},{3,2},{4,5},{5,4},{6,7},{7,6},{8,9},{9,8},{10,11... | collective-permute-start | bytes 1572872 | tf_op jit(solution)/shard_map/ppermute | solution.py:673
  234.1 20.9 %collective-permute-start.38 = (bf16[512,512]{1,0:T(8,128)(2,1)S(1)}, bf16[512,512]{1,0:T(8,128)(2,1)S(1)}, u32[]{:S(2)}, u32[]{:S(2)}) collective-permute-start(bf16[512,512]{1,0:T(8,128)(2,1)S(1)} %add_convert_fusion), channel_id=1, source_target_pairs={{0,2},{1,3},{2,0},{3,1},{4,6},{5,7},{6,4},{7,5},{8,10},{9,11},{10,... | collective-permute-start | bytes 1572872 | tf_op jit(solution)/shard_map/ppermute | solution.py:673
  235.1 53.3 %collective-permute-start.45 = (bf16[512,512]{1,0:T(8,128)(2,1)S(1)}, bf16[512,512]{1,0:T(8,128)(2,1)S(1)}, u32[]{:S(2)}, u32[]{:S(2)}) collective-permute-start(bf16[512,512]{1,0:T(8,128)(2,1)S(1)} %get-tuple-element.502.refs_3_), channel_id=1, source_target_pairs={{0,4},{4,0},{8,12},{12,8},{16,20},{20,16},{24,28},{28,24},{1,5},{5... | collective-permute-start | bytes 1572872 | tf_op jit(solution)/shard_map/ppermute | solution.py:673
  240.7 25.0 %collective-permute-start.41 = (bf16[2,256,512]{2,1,0:T(8,128)(2,1)S(1)}, bf16[2,256,512]{2,1,0:T(8,128)(2,1)S(1)}, u32[]{:S(2)}, u32[]{:S(2)}) collective-permute-start(bf16[2,256,512]{2,1,0:T(8,128)(2,1)S(1)} %bitcast.88), channel_id=1, source_target_pairs={{0,8},{4,12},{8,0},{12,4},{16,24},{20,28},{24,16},{28,20},{1,9},{5... | collective-permute-start | bytes 1572872 | tf_op jit(solution)/shard_map/ppermute | solution.py:673
  255.2 33.2 %collective-permute-start.43 = (bf16[2,256,512]{2,1,0:T(8,128)(2,1)S(1)}, bf16[2,256,512]{2,1,0:T(8,128)(2,1)S(1)}, u32[]{:S(2)}, u32[]{:S(2)}) collective-permute-start(bf16[2,256,512]{2,1,0:T(8,128)(2,1)S(1)} %bitcast.87), channel_id=1, source_target_pairs={{0,8},{4,12},{8,0},{12,4},{16,24},{20,28},{24,16},{28,20},{1,9},{5... | collective-permute-start | bytes 1572872 | tf_op jit(solution)/shard_map/ppermute | solution.py:673
  265.7 28.1 %collective-permute-start.44 = (bf16[2,256,512]{2,1,0:T(8,128)(2,1)S(1)}, bf16[2,256,512]{2,1,0:T(8,128)(2,1)S(1)}, u32[]{:S(2)}, u32[]{:S(2)}) collective-permute-start(bf16[2,256,512]{2,1,0:T(8,128)(2,1)S(1)} %bitcast.89), channel_id=1, source_target_pairs={{0,8},{4,12},{8,0},{12,4},{16,24},{20,28},{24,16},{28,20},{1,9},{5... | collective-permute-start | bytes 1572872 | tf_op jit(solution)/shard_map/ppermute | solution.py:673
  265.7 32.7 %collective-permute-start.46 = (bf16[4,96,1280]{2,1,0:T(8,128)(2,1)S(1)}, bf16[4,96,1280]{2,1,0:T(8,128)(2,1)S(1)}, u32[]{:S(2)}, u32[]{:S(2)}) collective-permute-start(bf16[4,96,1280]{2,1,0:T(8,128)(2,1)S(1)} %get-tuple-element.346), channel_id=1, source_target_pairs={{0,4},{4,0},{8,12},{12,8},{16,20},{20,16},{24,28},{28,24},{1,5},{5... | collective-permute-start | bytes 2949128 | tf_op jit(solution)/shard_map/ppermute | solution.py:673
  267.3 21.1 %collective-permute-start.42 = (bf16[1,256,512]{2,1,0:T(8,128)(2,1)S(1)}, bf16[1,256,512]{2,1,0:T(8,128)(2,1)S(1)}, u32[]{:S(2)}, u32[]{:S(2)}) collective-permute-start(bf16[1,256,512]{2,1,0:T(8,128)(2,1)S(1)} %get-tuple-element.328), channel_id=1, source_target_pairs={{0,16},{4,20},{8,24},{12,28},{16,0},{20,4},{24,8},{28,12},{1,17},{... | collective-permute-start | bytes 786440 | tf_op jit(solution)/shard_map/ppermute | solution.py:673
  298.6 28.8 %collective-permute-start.49 = (bf16[2,256,512]{2,1,0:T(8,128)(2,1)}, bf16[2,256,512]{2,1,0:T(8,128)(2,1)}, u32[]{:S(2)}, u32[]{:S(2)}) collective-permute-start(bf16[2,256,512]{2,1,0:T(8,128)(2,1)} %bitcast.23), channel_id=1, source_target_pairs={{0,8},{4,12},{8,0},{12,4},{16,24},{20,28},{24,16},{28,20},{1,9},{5... | collective-permute-start | bytes 1572872 | tf_op jit(solution)/shard_map/ppermute | solution.py:673
  300.1 27.3 %collective-permute-start.47 = (bf16[1,256,512]{2,1,0:T(8,128)(2,1)}, bf16[1,256,512]{2,1,0:T(8,128)(2,1)}, u32[]{:S(2)}, u32[]{:S(2)}) collective-permute-start(bf16[1,256,512]{2,1,0:T(8,128)(2,1)} %copy-done.81), channel_id=1, source_target_pairs={{0,16},{4,20},{8,24},{12,28},{16,0},{20,4},{24,8},{28,12},{1,17},{... | collective-permute-start | bytes 786440 | tf_op jit(solution)/shard_map/ppermute | solution.py:673
  302.9 24.5 %collective-permute-start.48 = (bf16[1,256,512]{2,1,0:T(8,128)(2,1)}, bf16[1,256,512]{2,1,0:T(8,128)(2,1)}, u32[]{:S(2)}, u32[]{:S(2)}) collective-permute-start(bf16[1,256,512]{2,1,0:T(8,128)(2,1)} %copy-done.80), channel_id=1, source_target_pairs={{0,16},{4,20},{8,24},{12,28},{16,0},{20,4},{24,8},{28,12},{1,17},{... | collective-permute-start | bytes 786440 | tf_op jit(solution)/shard_map/ppermute | solution.py:673
  305.3 22.1 %collective-permute-start.50 = (bf16[144,768]{1,0:T(8,128)(2,1)}, bf16[144,768]{1,0:T(8,128)(2,1)S(1)}, u32[]{:S(2)}, u32[]{:S(2)}) collective-permute-start(bf16[144,768]{1,0:T(8,128)(2,1)} %convert_add_fusion.3), channel_id=1, source_target_pairs={{0,8},{4,12},{8,0},{12,4},{16,24},{20,28},{24,16},{28,20},{1,9},{5... | collective-permute-start | bytes 663560 | tf_op jit(solution)/shard_map/ppermute | solution.py:673
  307.4 37.2 %collective-permute-start.52 = (bf16[2,96,1280]{2,1,0:T(8,128)(2,1)S(1)}, bf16[2,96,1280]{2,1,0:T(8,128)(2,1)S(1)}, u32[]{:S(2)}, u32[]{:S(2)}) collective-permute-start(bf16[2,96,1280]{2,1,0:T(8,128)(2,1)S(1)} %copy-done.69), channel_id=1, source_target_pairs={{0,8},{4,12},{8,0},{12,4},{16,24},{20,28},{24,16},{28,20},{1,9},{5... | collective-permute-start | bytes 1474568 | tf_op jit(solution)/shard_map/ppermute | solution.py:673
  329.5 21.4 %collective-permute-start.62 = (bf16[144,768]{1,0:T(8,128)(2,1)S(1)}, bf16[144,768]{1,0:T(8,128)(2,1)S(1)}, u32[]{:S(2)}, u32[]{:S(2)}) collective-permute-start(bf16[144,768]{1,0:T(8,128)(2,1)S(1)} %add_convert_fusion.2), channel_id=1, source_target_pairs={{0,16},{4,20},{8,24},{12,28},{16,0},{20,4},{24,8},{28,12},{1,17},{... | collective-permute-start | bytes 663560 | tf_op jit(solution)/shard_map/ppermute | solution.py:673
  330.7 32.8 %collective-permute-start.65 = (bf16[1,96,1536]{2,1,0:T(8,128)(2,1)S(1)}, bf16[1,96,1536]{2,1,0:T(8,128)(2,1)S(1)}, u32[]{:S(2)}, u32[]{:S(2)}) collective-permute-start(bf16[1,96,1536]{2,1,0:T(8,128)(2,1)S(1)} %get-tuple-element.398), channel_id=1, source_target_pairs={{0,4},{4,0},{8,12},{12,8},{16,20},{20,16},{24,28},{28,24},{1,5},{5... | collective-permute-start | bytes 884744 | tf_op jit(solution)/shard_map/ppermute | solution.py:673
  332.6 25.9 %collective-permute-start.60 = (bf16[1,256,512]{2,1,0:T(8,128)(2,1)S(1)}, bf16[1,256,512]{2,1,0:T(8,128)(2,1)S(1)}, u32[]{:S(2)}, u32[]{:S(2)}) collective-permute-start(bf16[1,256,512]{2,1,0:T(8,128)(2,1)S(1)} %get-tuple-element.386), channel_id=1, source_target_pairs={{0,16},{4,20},{8,24},{12,28},{16,0},{20,4},{24,8},{28,12},{1,17},{... | collective-permute-start | bytes 786440 | tf_op jit(solution)/shard_map/ppermute | solution.py:673
  350.1 25.4 %collective-permute-start.61 = (bf16[1,96,1280]{2,1,0:T(8,128)(2,1)S(1)}, bf16[1,96,1280]{2,1,0:T(8,128)(2,1)S(1)}, u32[]{:S(2)}, u32[]{:S(2)}) collective-permute-start(bf16[1,96,1280]{2,1,0:T(8,128)(2,1)S(1)} %get-tuple-element.394), channel_id=1, source_target_pairs={{0,16},{4,20},{8,24},{12,28},{16,0},{20,4},{24,8},{28,12},{1,17},{... | collective-permute-start | bytes 737288 | tf_op jit(solution)/shard_map/ppermute | solution.py:673
  351.6 25.9 %collective-permute-start.63 = (bf16[128,768]{1,0:T(8,128)(2,1)S(1)}, bf16[128,768]{1,0:T(8,128)(2,1)S(1)}, u32[]{:S(2)}, u32[]{:S(2)}) collective-permute-start(bf16[128,768]{1,0:T(8,128)(2,1)S(1)} %slice.296), channel_id=1, source_target_pairs={{0,2},{1,3},{2,0},{3,1},{4,6},{5,7},{6,4},{7,5},{8,10},{9,11},{10,... | collective-permute-start | bytes 589832 | tf_op jit(solution)/shard_map/ppermute | solution.py:673
  358.5 21.4 %collective-permute-start.59 = (bf16[128,512]{1,0:T(8,128)(2,1)S(1)}, bf16[128,512]{1,0:T(8,128)(2,1)S(1)}, u32[]{:S(2)}, u32[]{:S(2)}) collective-permute-start(bf16[128,512]{1,0:T(8,128)(2,1)S(1)} %add_convert_fusion.3), channel_id=1, source_target_pairs={{0,16},{4,20},{8,24},{12,28},{16,0},{20,4},{24,8},{28,12},{1,17},{... | collective-permute-start | bytes 393224 | tf_op jit(solution)/shard_map/ppermute | solution.py:673
  (145 other events, 1057.9 us)

commit v2 on v1

--- a/solution.py
+++ b/solution.py
@@ -325,8 +325,9 @@
 
 def level_kernel(
     places, own_w, near_w, mid_w, far_w, own, near, mid, far, carried, bias,
-    transform_out, gate_out, carried_out, low_out, *peers_out,
+    transform_out, gate_out, low_out, *rest_out,
 ):
+    peers_out = rest_out[len(rest_out) % 2 :]
     if peers_out:
         ours, theirs = peers_out
         size = own.shape[1] * 4 // (places.shape[0] - 4)
@@ -356,8 +357,9 @@
     opened = 1.0 / (1.0 + jnp.exp(-gate))
     swished = transform / (1.0 + jnp.exp(-transform))
     mixed = opened * swished + (1.0 - opened) * carried[...].astype(F32)
-    carried_out[...] = mixed
     low_out[...] = mixed.astype(BF16)
+    if len(rest_out) % 2:
+        rest_out[0][...] = mixed
 
 
 def level_back_kernel(places, far_w, mid_w, transform, gate, carried, grad, both_out, carry_out, bias_out, far_out, mid_out):
@@ -777,15 +779,17 @@
         far_peer = pltpu.HBM(peer_shape.shape, BF16)
         far_f32 = pltpu.HBM(square, F32)
         direct = (CHANNELS // dp_count) % 128 == 0
-        transform, gate, mixed_state, inputs, *peer_blocks = level_call(
+        more = depth + 1 < LAYERS
+        transform, gate, inputs, *peer_blocks = level_call(
             level_kernel,
             places,
             depth,
             (0, 1, 2, 3),
             weights,
             (a, b, c, d, carried, highway_bias[depth]),
-            [far_f32, far_f32, wide_f32, wide_bf16] + [far_peer, peer_shape] * direct,
+            [far_f32, far_f32, wide_bf16] + [wide_f32] * more + [far_peer, peer_shape] * direct,
         )
+        mixed_state = peer_blocks.pop(0) if more else None
         if direct:
             ours, theirs = peer_blocks
         else:

time: 392 us -> 392 us (level)
  waiting for transfers between devices: 132 us -> 122 us
  starting transfers between devices: 66 us -> 72.6 us
    ppermute x66, waiting for transfers between devices: 128 us -> 118 us  [swap(): return lax.ppermute(values, axis, [(i, i ^ bit) for i in range(count)])]
    ppermute x66, starting transfers between devices: 59.6 us -> 66.2 us  [swap(): return lax.ppermute(values, axis, [(i, i ^ bit) for i in range(count)])]
  transfers between devices with their start and end apart: 67 -> 67, of which waited for: 35 -> 34; matrix products, arithmetic and copies ran while one was open for 9% -> 9% of each run, Pallas kernels for 18% -> 19%
where the time goes in v2:
time: 392 us; the launch traced here: 384 us
  Pallas kernels  126 us (32%)
  waiting for transfers between devices  122 us (31%)
  starting transfers between devices  72.6 us (19%)
  local copies, waits for them, and re-layouts  46.3 us (12%)
  other arithmetic  12.4 us (3%)
    ppermute x66, waiting for transfers between devices, swap(): return lax.ppermute(values, axis, [(i, i ^ bit) for i in range(count)])  118 us
    ppermute x66, starting transfers between devices, swap(): return lax.ppermute(values, axis, [(i, i ^ bit) for i in range(count)])  66.2 us
    pallas_call x2, Pallas kernels, cnn_backward(): pl.pallas_call(kernel, in_specs=[pl.BlockSpec(memory_space=pltpu.SMEM)] +...  37.1 us
    pallas_call x24, Pallas kernels, local_call(): pl.pallas_call(kernel, in_specs=specs, out_specs=[vm] * len(shapes), out_...  34.6 us
    pallas_call x6, Pallas kernels, level_call(): pl.pallas_call(kernel, grid_spec=pltpu.PrefetchScalarGridSpec(num_scalar_...  30.4 us
    unnamed x212, local copies, waits for them, and re-layouts  23.5 us
    pallas_call x1, Pallas kernels, cnn_forward(): pl.pallas_call(functools.partial(forward_kernel, block), in_specs=[pl.Blo...  19.8 us
    optimization_barrier x1, local copies, waits for them, and re-layouts, fence(): return lax.optimization_barrier(values)  8.19 us
  transfers between devices with their start and end apart: 67, of which 34 were waited for; matrix products, arithmetic and copies ran while one was open for 9% of the time, Pallas kernels for 19%

profile of v2, /device:TPU:1, one launch (start us, length us, event | category | flops | bytes accessed | tf_op | source)
XLA Modules:
  0.0 384.5 jit_solution(14394866554399728063)
XLA Ops:
  3.8 6.4 %all-to-all-start = ((s32[8,1,3200]{2,1,0:T(1,128)}), s32[8,1,3200]{2,1,0:T(1,128)S(1)}, u32[]{:S(2)}, u32[]{:S(2)}) async-start(s32[8,1,3200]{2,1,0:T(1,128)} %all_to_all.8), calls=%async_computation | async-start | bytes 204800 | tf_op jit(solution)/shard_map/all_to_all | solution.py:743
  12.3 4.1 %all-to-all-done = s32[8,1,3200]{2,1,0:T(1,128)S(1)} async-done(((s32[8,1,3200]{2,1,0:T(1,128)}), s32[8,1,3200]{2,1,0:T(1,128)S(1)}, u32[]{:S(2)}, u32[]{:S(2)}) %all-to-all-start) | async-done | bytes 102432 | tf_op jit(solution)/shard_map/all_to_all | solution.py:743
  21.3 19.8 %shard_map.393 = (bf16[512,512]{1,0:T(8,128)(2,1)}, bf16[8,512,128]{2,1,0:T(8,128)(2,1)S(1)}) custom-call(s32[11]{0:T(128)S(1)} %pad_add_fusion.2.counts, s32[7,512,8]{2,1,0:T(8,128)S(1)} %bitcast.75, bf16[2176,128]{1,0:T(8,128)(2,1)S(1)} %copy-done.12, bf16[112,512]{1,0:T(8,128)(2,1)S(1)} %compare_select_fusion.1.filters_ref, f32[1,512]{1,0:T(1,128)S(1)} %bitcast.84), custom_call_target="tpu_custom_call" | custom-call | flops 1 | bytes 1 | tf_op jit(solution)/shard_map/pallas_call | solution.py:113
  45.6 8.2 %copy.126 = bf16[2,2048,2,512]{3,1,2,0:T(8,128)(2,1)} copy(bf16[2,2048,2,512]{3,2,1,0:T(2,128)(2,1)} %param.33) | data formatting | bytes 16777216 | tf_op jit(solution)/shard_map/optimization_barrier | solution.py:670
  58.2 7.3 %shard_map.394 = (f32[512,512]{1,0:T(8,128)}, f32[512,512]{1,0:T(8,128)}, bf16[512,512]{1,0:T(8,128)(2,1)S(1)}, f32[512,512]{1,0:T(8,128)S(1)}, bf16[512,1024]{1...) custom-call(s32[12]{0:T(128)S(1)} %pad_add_fusion.1.places, bf16[2,2,2048,512]{3,2,1,0:T(8,128)(2,1)} %bitcast.90, ...), custom_call_target="tpu_custom_call" | custom-call | flops 1 | bytes 1 | tf_op jit(solution)/shard_map/pallas_call | solution.py:312
  69.1 8.6 %collective-permute-done.5.refs_0_ = bf16[176,1024]{1,0:T(8,128)(2,1)S(1)} collective-permute-done((bf16[176,1024]{1,0:T(8,128)(2,1)S(1)}, bf16[176,1024]{1,0:T(8,128)(2,1)S(1)}, u32[]{:S(2)}, u32[]{:S(2)}) %collective-permute-start.5) | collective-permute-done | bytes 360480 | tf_op jit(solution)/shard_map/ppermute | solution.py:675
  84.7 7.5 %shard_map.395 = (f32[512,512]{1,0:T(8,128)}, f32[512,512]{1,0:T(8,128)}, bf16[512,512]{1,0:T(8,128)(2,1)S(1)}, bf16[512,1024]{1,0:T(8,128)(2,1)}, bf16[512,1024]{1,0:T(8,128)(2,1)S(1)}) custom-call(s32[12]{0:T(128)S(1)} %pad_add_fusion.1.places, bf16[2,2,2048,512]{3,2,1,0:T(8,128)(2,1)} %bitcast.94, bf16[2,2,2048,512]{3,2,1,0:T(8,128)(2,1)} %bitcast.95, ...), custom_call_target="tpu_custom_call" | custom-call | flops 1 | bytes 1 | tf_op jit(solution)/shard_map/pallas_call | solution.py:312
  98.4 5.4 %collective-permute-done.9.refs_1_ = bf16[176,1024]{1,0:T(8,128)(2,1)} collective-permute-done((bf16[176,1024]{1,0:T(8,128)(2,1)}, bf16[176,1024]{1,0:T(8,128)(2,1)}, u32[]{:S(2)}, u32[]{:S(2)}) %collective-permute-start.9) | collective-permute-done | bytes 360480 | tf_op jit(solution)/shard_map/ppermute | solution.py:675
  117.2 8.4 %collective-permute-done.13.refs_2_ = bf16[160,1024]{1,0:T(8,128)(2,1)S(1)} collective-permute-done((bf16[160,1024]{1,0:T(8,128)(2,1)S(1)}, bf16[160,1024]{1,0:T(8,128)(2,1)S(1)}, u32[]{:S(2)}, u32[]{:S(2)}) %collective-permute-start.13) | collective-permute-done | bytes 327712 | tf_op jit(solution)/shard_map/ppermute | solution.py:675
  134.4 8.9 %collective-permute-done.17.refs_0_ = bf16[176,1024]{1,0:T(8,128)(2,1)S(1)} collective-permute-done((bf16[176,1024]{1,0:T(8,128)(2,1)S(1)}, bf16[176,1024]{1,0:T(8,128)(2,1)S(1)}, u32[]{:S(2)}, u32[]{:S(2)}) %collective-permute-start.17) | collective-permute-done | bytes 360480 | tf_op jit(solution)/shard_map/ppermute | solution.py:675
  156.5 6.1 %collective-permute-done.21.refs_1_ = bf16[176,1024]{1,0:T(8,128)(2,1)S(1)} collective-permute-done((bf16[176,1024]{1,0:T(8,128)(2,1)S(1)}, bf16[176,1024]{1,0:T(8,128)(2,1)S(1)}, u32[]{:S(2)}, u32[]{:S(2)}) %collective-permute-start.21) | collective-permute-done | bytes 360480 | tf_op jit(solution)/shard_map/ppermute | solution.py:675
  166.3 4.1 %shard_map.405 = (bf16[512,576]{1,0:T(8,128)(2,1)S(1)}, f32[1,576]{1,0:T(1,128)S(1)}, bf16[256,768]{1,0:T(8,128)(2,1)S(1)}) custom-call(bf16[256,768]{1,0:T(8,128)(2,1)S(1)} %get-tuple-element.252.own.refs_3_, bf16[256,768]{1,0:T(8,128)(2,1)S(1)} %collective-permute-done.23.other.refs_4_, bf16[192,768]{1,0:T(8,128)(2,1)S(1)} %copy-done.11, ...), custom_call_target="tpu_custom_call" | custom-call | flops 1 | bytes 1 | tf_op jit(solution)/shard_map/pallas_call | solution.py:414
  173.6 8.4 %collective-permute-done.26.refs_2_ = bf16[160,1024]{1,0:T(8,128)(2,1)S(1)} collective-permute-done((bf16[160,1024]{1,0:T(8,128)(2,1)S(1)}, bf16[160,1024]{1,0:T(8,128)(2,1)S(1)}, u32[]{:S(2)}, u32[]{:S(2)}) %collective-permute-start.26) | collective-permute-done | bytes 327712 | tf_op jit(solution)/shard_map/ppermute | solution.py:675
  187.5 4.5 %shard_map.408 = (bf16[512,1024]{1,0:T(8,128)(2,1)S(1)}, f32[512,512]{1,0:T(8,128)S(1)}, f32[1,1024]{1,0:T(1,128)S(1)}, bf16[512,512]{1,0:T(8,128)(2,1)}, f32[512,512]{1,0:T(8,128)S(1)}) custom-call(s32[12]{0:T(128)S(1)} %pad_add_fusion.1.places, bf16[2,2,2048,512]{3,2,1,0:T(8,128)(2,1)} %bitcast.98, bf16[2,2,2048,512]{3,2,1,0:T(8,128)(2,1)} %bitcast.99, ...), custom_call_target="tpu_custom_call" | custom-call | flops 1 | bytes 1 | tf_op jit(solution)/shard_map/pallas_call | solution.py:312
  202.9 4.3 %shard_map.410 = (bf16[4,96,1280]{2,1,0:T(8,128)(2,1)S(1)}, bf16[4,96,1280]{2,1,0:T(8,128)(2,1)S(1)}) custom-call(s32[8]{0:T(128)S(1)} %select_reduce_fusion.1.spots, bf16[256,768]{1,0:T(8,128)(2,1)S(1)} %copy-done.45, bf16[256,768]{1,0:T(8,128)(2,1)S(1)} %copy-done.47, bf16[512,576]{1,0:T(8,128)(2,1)S(1)} %copy-done.67, bf16[256,768]{1,0:T(8,128)(2,1)S(1)} %copy-done.41, ...), custom_call_target="tpu_custom_call" | custom-call | flops 4000000000 | bytes 10000000 | tf_op jit(solution)/shard_map/pallas_call | solution.py:414
  207.2 6.0 %collective-permute-done.33.refs_2_ = bf16[4,96,1024]{2,1,0:T(8,128)(2,1)S(1)} collective-permute-done((bf16[4,96,1024]{2,1,0:T(8,128)(2,1)}, bf16[4,96,1024]{2,1,0:T(8,128)(2,1)S(1)}, u32[]{:S(2)}, u32[]{:S(2)}) %collective-permute-start.33) | collective-permute-done | bytes 786464 | tf_op jit(solution)/shard_map/ppermute | solution.py:675
  213.2 6.2 %collective-permute-done.32.refs_4_ = bf16[512,1024]{1,0:T(8,128)(2,1)S(1)} collective-permute-done((bf16[512,1024]{1,0:T(8,128)(2,1)S(1)}, bf16[512,1024]{1,0:T(8,128)(2,1)S(1)}, u32[]{:S(2)}, u32[]{:S(2)}) %collective-permute-start.32) | collective-permute-done | bytes 1048608 | tf_op jit(solution)/shard_map/ppermute | solution.py:675
  242.1 13.5 %collective-permute-done.40.refs_1_ = bf16[2,96,1536]{2,1,0:T(8,128)(2,1)S(1)} collective-permute-done((bf16[2,96,1536]{2,1,0:T(8,128)(2,1)S(1)}, bf16[2,96,1536]{2,1,0:T(8,128)(2,1)S(1)}, u32[]{:S(2)}, u32[]{:S(2)}) %collective-permute-start.40) | collective-permute-done | bytes 589856 | tf_op jit(solution)/shard_map/ppermute | solution.py:675
  259.1 5.9 %collective-permute-done.41.refs_1_ = bf16[2,256,512]{2,1,0:T(8,128)(2,1)S(1)} collective-permute-done((bf16[2,256,512]{2,1,0:T(8,128)(2,1)S(1)}, bf16[2,256,512]{2,1,0:T(8,128)(2,1)S(1)}, u32[]{:S(2)}, u32[]{:S(2)}) %collective-permute-start.41) | collective-permute-done | bytes 524320 | tf_op jit(solution)/shard_map/ppermute | solution.py:675
  270.1 18.5 %shard_map.417 = (f32[112,256]{1,0:T(8,128)S(1)}, f32[1,256]{1,0:T(1,128)S(1)}, f32[8,512,128]{2,1,0:T(8,128)S(1)}) custom-call(s32[11]{0:T(128)S(1)} %pad_add_fusion.2.counts, bf16[8,512,128]{2,1,0:T(8,128)(2,1)S(1)} %copy-done.9, bf16[112,256]{1,0:T(8,128)(2,1)S(1)} %get-tuple-element.526.filters, f32[1,256]{1,0:T(1,128)S(1)} %bitcast.86, ...), custom_call_target="tpu_custom_call" | custom-call | flops 1 | bytes 1 | tf_op jit(solution)/shard_map/pallas_call | solution.py:231
  307.9 18.6 %shard_map.422 = (f32[112,256]{1,0:T(8,128)S(1)}, f32[1,256]{1,0:T(1,128)S(1)}, f32[8,512,128]{2,1,0:T(8,128)S(1)}) custom-call(s32[11]{0:T(128)S(1)} %pad_add_fusion.2.counts, bf16[8,512,128]{2,1,0:T(8,128)(2,1)S(1)} %copy-done.9, bf16[112,256]{1,0:T(8,128)(2,1)S(1)} %copy-done.53, f32[1,256]{1,0:T(1,128)S(1)} %bitcast.85, ...), custom_call_target="tpu_custom_call" | custom-call | flops 1 | bytes 1 | tf_op jit(solution)/shard_map/pallas_call | solution.py:231
  333.8 4.4 %shard_map.424 = f32[40,128]{1,0:T(8,128)S(1)} custom-call(s32[50,512]{1,0:T(8,128)S(1)} %bitcast.79, f32[8,512,128]{2,1,0:T(8,128)S(1)} %get-tuple-element.366.embed_grad), custom_call_target="tpu_custom_call" | custom-call | flops 1 | bytes 1 | tf_op jit(solution)/shard_map/pallas_call | solution.py:282
  338.2 4.9 %collective-permute-done.52.refs_1_ = bf16[2,96,1280]{2,1,0:T(8,128)(2,1)S(1)} collective-permute-done((bf16[2,96,1280]{2,1,0:T(8,128)(2,1)S(1)}, bf16[2,96,1280]{2,1,0:T(8,128)(2,1)S(1)}, u32[]{:S(2)}, u32[]{:S(2)}) %collective-permute-start.52) | collective-permute-done | bytes 491552 | tf_op jit(solution)/shard_map/ppermute | solution.py:675
  372.8 6.6 %collective-permute-start.64 = (bf16[256,768]{1,0:T(8,128)(2,1)S(1)}, bf16[256,768]{1,0:T(8,128)(2,1)S(1)}, u32[]{:S(2)}, u32[]{:S(2)}) collective-permute-start(bf16[256,768]{1,0:T(8,128)(2,1)S(1)} %pad_maximum_fusion.4), channel_id=1, source_target_pairs={{0,1},{1,0},{2,3},{3,2},{4,5},{5,4},{6,7},{7,6},{8,9},{9,8},{10,11... | collective-permute-start | bytes 1179656 | tf_op jit(solution)/shard_map/ppermute | solution.py:675
  (481 shorter events, 185.5 us)
Async XLA Ops:
  193.9 19.2 %collective-permute-start.33 = (bf16[4,96,1024]{2,1,0:T(8,128)(2,1)}, bf16[4,96,1024]{2,1,0:T(8,128)(2,1)S(1)}, u32[]{:S(2)}, u32[]{:S(2)}) collective-permute-start(bf16[4,96,1024]{2,1,0:T(8,128)(2,1)} %copy-done.63), channel_id=1, source_target_pairs={{0,8},{4,12},{8,0},{12,4},{16,24},{20,28},{24,16},{28,20},{1,9},{5... | collective-permute-start | bytes 2359304 | tf_op jit(solution)/shard_map/ppermute | solution.py:675
  194.6 24.7 %collective-permute-start.32 = (bf16[512,1024]{1,0:T(8,128)(2,1)S(1)}, bf16[512,1024]{1,0:T(8,128)(2,1)S(1)}, u32[]{:S(2)}, u32[]{:S(2)}) collective-permute-start(bf16[512,1024]{1,0:T(8,128)(2,1)S(1)} %get-tuple-element.305.both.refs_3_), channel_id=1, source_target_pairs={{0,4},{4,0},{8,12},{12,8},{16,20},{20,16},{24,28},{28,24},{1,5},{5... | collective-permute-start | bytes 3145736 | tf_op jit(solution)/shard_map/ppermute | solution.py:675
  201.4 17.9 %collective-permute-start.30 = (bf16[512,512]{1,0:T(8,128)(2,1)S(1)}, bf16[512,512]{1,0:T(8,128)(2,1)S(1)}, u32[]{:S(2)}, u32[]{:S(2)}) collective-permute-start(bf16[512,512]{1,0:T(8,128)(2,1)S(1)} %get-tuple-element.269), channel_id=1, source_target_pairs={{0,1},{1,0},{2,3},{3,2},{4,5},{5,4},{6,7},{7,6},{8,9},{9,8},{10,11... | collective-permute-start | bytes 1572872 | tf_op jit(solution)/shard_map/ppermute | solution.py:675
  201.8 17.5 %collective-permute-start.31 = (bf16[512,512]{1,0:T(8,128)(2,1)S(1)}, bf16[512,512]{1,0:T(8,128)(2,1)S(1)}, u32[]{:S(2)}, u32[]{:S(2)}) collective-permute-start(bf16[512,512]{1,0:T(8,128)(2,1)S(1)} %add_convert_fusion.1), channel_id=1, source_target_pairs={{0,2},{1,3},{2,0},{3,1},{4,6},{5,7},{6,4},{7,5},{8,10},{9,11},{10,... | collective-permute-start | bytes 1572872 | tf_op jit(solution)/shard_map/ppermute | solution.py:675
  227.0 28.6 %collective-permute-start.40 = (bf16[2,96,1536]{2,1,0:T(8,128)(2,1)S(1)}, bf16[2,96,1536]{2,1,0:T(8,128)(2,1)S(1)}, u32[]{:S(2)}, u32[]{:S(2)}) collective-permute-start(bf16[2,96,1536]{2,1,0:T(8,128)(2,1)S(1)} %get-tuple-element.303), channel_id=1, source_target_pairs={{0,16},{4,20},{8,24},{12,28},{16,0},{20,4},{24,8},{28,12},{1,17},{... | collective-permute-start | bytes 1769480 | tf_op jit(solution)/shard_map/ppermute | solution.py:675
  233.6 22.0 %collective-permute-start.37 = (bf16[512,512]{1,0:T(8,128)(2,1)S(1)}, bf16[512,512]{1,0:T(8,128)(2,1)S(1)}, u32[]{:S(2)}, u32[]{:S(2)}) collective-permute-start(bf16[512,512]{1,0:T(8,128)(2,1)S(1)} %get-tuple-element.297), channel_id=1, source_target_pairs={{0,1},{1,0},{2,3},{3,2},{4,5},{5,4},{6,7},{7,6},{8,9},{9,8},{10,11... | collective-permute-start | bytes 1572872 | tf_op jit(solution)/shard_map/ppermute | solution.py:675
  234.2 21.4 %collective-permute-start.38 = (bf16[512,512]{1,0:T(8,128)(2,1)S(1)}, bf16[512,512]{1,0:T(8,128)(2,1)S(1)}, u32[]{:S(2)}, u32[]{:S(2)}) collective-permute-start(bf16[512,512]{1,0:T(8,128)(2,1)S(1)} %add_convert_fusion), channel_id=1, source_target_pairs={{0,2},{1,3},{2,0},{3,1},{4,6},{5,7},{6,4},{7,5},{8,10},{9,11},{10,... | collective-permute-start | bytes 1572872 | tf_op jit(solution)/shard_map/ppermute | solution.py:675
  235.2 54.1 %collective-permute-start.45 = (bf16[512,512]{1,0:T(8,128)(2,1)S(1)}, bf16[512,512]{1,0:T(8,128)(2,1)S(1)}, u32[]{:S(2)}, u32[]{:S(2)}) collective-permute-start(bf16[512,512]{1,0:T(8,128)(2,1)S(1)} %get-tuple-element.502.refs_3_), channel_id=1, source_target_pairs={{0,4},{4,0},{8,12},{12,8},{16,20},{20,16},{24,28},{28,24},{1,5},{5... | collective-permute-start | bytes 1572872 | tf_op jit(solution)/shard_map/ppermute | solution.py:675
  240.7 24.3 %collective-permute-start.41 = (bf16[2,256,512]{2,1,0:T(8,128)(2,1)S(1)}, bf16[2,256,512]{2,1,0:T(8,128)(2,1)S(1)}, u32[]{:S(2)}, u32[]{:S(2)}) collective-permute-start(bf16[2,256,512]{2,1,0:T(8,128)(2,1)S(1)} %bitcast.88), channel_id=1, source_target_pairs={{0,8},{4,12},{8,0},{12,4},{16,24},{20,28},{24,16},{28,20},{1,9},{5... | collective-permute-start | bytes 1572872 | tf_op jit(solution)/shard_map/ppermute | solution.py:675
  255.8 33.5 %collective-permute-start.43 = (bf16[2,256,512]{2,1,0:T(8,128)(2,1)S(1)}, bf16[2,256,512]{2,1,0:T(8,128)(2,1)S(1)}, u32[]{:S(2)}, u32[]{:S(2)}) collective-permute-start(bf16[2,256,512]{2,1,0:T(8,128)(2,1)S(1)} %bitcast.87), channel_id=1, source_target_pairs={{0,8},{4,12},{8,0},{12,4},{16,24},{20,28},{24,16},{28,20},{1,9},{5... | collective-permute-start | bytes 1572872 | tf_op jit(solution)/shard_map/ppermute | solution.py:675
  265.0 28.1 %collective-permute-start.44 = (bf16[2,256,512]{2,1,0:T(8,128)(2,1)S(1)}, bf16[2,256,512]{2,1,0:T(8,128)(2,1)S(1)}, u32[]{:S(2)}, u32[]{:S(2)}) collective-permute-start(bf16[2,256,512]{2,1,0:T(8,128)(2,1)S(1)} %bitcast.89), channel_id=1, source_target_pairs={{0,8},{4,12},{8,0},{12,4},{16,24},{20,28},{24,16},{28,20},{1,9},{5... | collective-permute-start | bytes 1572872 | tf_op jit(solution)/shard_map/ppermute | solution.py:675
  265.0 32.7 %collective-permute-start.46 = (bf16[4,96,1280]{2,1,0:T(8,128)(2,1)S(1)}, bf16[4,96,1280]{2,1,0:T(8,128)(2,1)S(1)}, u32[]{:S(2)}, u32[]{:S(2)}) collective-permute-start(bf16[4,96,1280]{2,1,0:T(8,128)(2,1)S(1)} %get-tuple-element.346), channel_id=1, source_target_pairs={{0,4},{4,0},{8,12},{12,8},{16,20},{20,16},{24,28},{28,24},{1,5},{5... | collective-permute-start | bytes 2949128 | tf_op jit(solution)/shard_map/ppermute | solution.py:675
  266.7 22.6 %collective-permute-start.42 = (bf16[1,256,512]{2,1,0:T(8,128)(2,1)S(1)}, bf16[1,256,512]{2,1,0:T(8,128)(2,1)S(1)}, u32[]{:S(2)}, u32[]{:S(2)}) collective-permute-start(bf16[1,256,512]{2,1,0:T(8,128)(2,1)S(1)} %get-tuple-element.328), channel_id=1, source_target_pairs={{0,16},{4,20},{8,24},{12,28},{16,0},{20,4},{24,8},{28,12},{1,17},{... | collective-permute-start | bytes 786440 | tf_op jit(solution)/shard_map/ppermute | solution.py:675
  297.9 28.6 %collective-permute-start.49 = (bf16[2,256,512]{2,1,0:T(8,128)(2,1)}, bf16[2,256,512]{2,1,0:T(8,128)(2,1)}, u32[]{:S(2)}, u32[]{:S(2)}) collective-permute-start(bf16[2,256,512]{2,1,0:T(8,128)(2,1)} %bitcast.23), channel_id=1, source_target_pairs={{0,8},{4,12},{8,0},{12,4},{16,24},{20,28},{24,16},{28,20},{1,9},{5... | collective-permute-start | bytes 1572872 | tf_op jit(solution)/shard_map/ppermute | solution.py:675
  299.4 27.1 %collective-permute-start.47 = (bf16[1,256,512]{2,1,0:T(8,128)(2,1)}, bf16[1,256,512]{2,1,0:T(8,128)(2,1)}, u32[]{:S(2)}, u32[]{:S(2)}) collective-permute-start(bf16[1,256,512]{2,1,0:T(8,128)(2,1)} %copy-done.81), channel_id=1, source_target_pairs={{0,16},{4,20},{8,24},{12,28},{16,0},{20,4},{24,8},{28,12},{1,17},{... | collective-permute-start | bytes 786440 | tf_op jit(solution)/shard_map/ppermute | solution.py:675
  302.7 23.8 %collective-permute-start.48 = (bf16[1,256,512]{2,1,0:T(8,128)(2,1)}, bf16[1,256,512]{2,1,0:T(8,128)(2,1)}, u32[]{:S(2)}, u32[]{:S(2)}) collective-permute-start(bf16[1,256,512]{2,1,0:T(8,128)(2,1)} %copy-done.80), channel_id=1, source_target_pairs={{0,16},{4,20},{8,24},{12,28},{16,0},{20,4},{24,8},{28,12},{1,17},{... | collective-permute-start | bytes 786440 | tf_op jit(solution)/shard_map/ppermute | solution.py:675
  305.1 21.3 %collective-permute-start.50 = (bf16[144,768]{1,0:T(8,128)(2,1)}, bf16[144,768]{1,0:T(8,128)(2,1)S(1)}, u32[]{:S(2)}, u32[]{:S(2)}) collective-permute-start(bf16[144,768]{1,0:T(8,128)(2,1)} %convert_add_fusion.3), channel_id=1, source_target_pairs={{0,8},{4,12},{8,0},{12,4},{16,24},{20,28},{24,16},{28,20},{1,9},{5... | collective-permute-start | bytes 663560 | tf_op jit(solution)/shard_map/ppermute | solution.py:675
  306.6 36.5 %collective-permute-start.52 = (bf16[2,96,1280]{2,1,0:T(8,128)(2,1)S(1)}, bf16[2,96,1280]{2,1,0:T(8,128)(2,1)S(1)}, u32[]{:S(2)}, u32[]{:S(2)}) collective-permute-start(bf16[2,96,1280]{2,1,0:T(8,128)(2,1)S(1)} %copy-done.69), channel_id=1, source_target_pairs={{0,8},{4,12},{8,0},{12,4},{16,24},{20,28},{24,16},{28,20},{1,9},{5... | collective-permute-start | bytes 1474568 | tf_op jit(solution)/shard_map/ppermute | solution.py:675
  328.1 22.2 %collective-permute-start.62 = (bf16[144,768]{1,0:T(8,128)(2,1)S(1)}, bf16[144,768]{1,0:T(8,128)(2,1)S(1)}, u32[]{:S(2)}, u32[]{:S(2)}) collective-permute-start(bf16[144,768]{1,0:T(8,128)(2,1)S(1)} %add_convert_fusion.2), channel_id=1, source_target_pairs={{0,16},{4,20},{8,24},{12,28},{16,0},{20,4},{24,8},{28,12},{1,17},{... | collective-permute-start | bytes 663560 | tf_op jit(solution)/shard_map/ppermute | solution.py:675
  330.4 32.4 %collective-permute-start.65 = (bf16[1,96,1536]{2,1,0:T(8,128)(2,1)S(1)}, bf16[1,96,1536]{2,1,0:T(8,128)(2,1)S(1)}, u32[]{:S(2)}, u32[]{:S(2)}) collective-permute-start(bf16[1,96,1536]{2,1,0:T(8,128)(2,1)S(1)} %get-tuple-element.398), channel_id=1, source_target_pairs={{0,4},{4,0},{8,12},{12,8},{16,20},{20,16},{24,28},{28,24},{1,5},{5... | collective-permute-start | bytes 884744 | tf_op jit(solution)/shard_map/ppermute | solution.py:675
  332.5 25.3 %collective-permute-start.60 = (bf16[1,256,512]{2,1,0:T(8,128)(2,1)S(1)}, bf16[1,256,512]{2,1,0:T(8,128)(2,1)S(1)}, u32[]{:S(2)}, u32[]{:S(2)}) collective-permute-start(bf16[1,256,512]{2,1,0:T(8,128)(2,1)S(1)} %get-tuple-element.386), channel_id=1, source_target_pairs={{0,16},{4,20},{8,24},{12,28},{16,0},{20,4},{24,8},{28,12},{1,17},{... | collective-permute-start | bytes 786440 | tf_op jit(solution)/shard_map/ppermute | solution.py:675
  349.4 21.3 %collective-permute-start.61 = (bf16[1,96,1280]{2,1,0:T(8,128)(2,1)S(1)}, bf16[1,96,1280]{2,1,0:T(8,128)(2,1)S(1)}, u32[]{:S(2)}, u32[]{:S(2)}) collective-permute-start(bf16[1,96,1280]{2,1,0:T(8,128)(2,1)S(1)} %get-tuple-element.394), channel_id=1, source_target_pairs={{0,16},{4,20},{8,24},{12,28},{16,0},{20,4},{24,8},{28,12},{1,17},{... | collective-permute-start | bytes 737288 | tf_op jit(solution)/shard_map/ppermute | solution.py:675
  351.0 21.7 %collective-permute-start.63 = (bf16[128,768]{1,0:T(8,128)(2,1)S(1)}, bf16[128,768]{1,0:T(8,128)(2,1)S(1)}, u32[]{:S(2)}, u32[]{:S(2)}) collective-permute-start(bf16[128,768]{1,0:T(8,128)(2,1)S(1)} %slice.296), channel_id=1, source_target_pairs={{0,2},{1,3},{2,0},{3,1},{4,6},{5,7},{6,4},{7,5},{8,10},{9,11},{10,... | collective-permute-start | bytes 589832 | tf_op jit(solution)/shard_map/ppermute | solution.py:675
  357.8 22.3 %collective-permute-start.59 = (bf16[128,512]{1,0:T(8,128)(2,1)S(1)}, bf16[128,512]{1,0:T(8,128)(2,1)S(1)}, u32[]{:S(2)}, u32[]{:S(2)}) collective-permute-start(bf16[128,512]{1,0:T(8,128)(2,1)S(1)} %add_convert_fusion.3), channel_id=1, source_target_pairs={{0,16},{4,20},{8,24},{12,28},{16,0},{20,4},{24,8},{28,12},{1,17},{... | collective-permute-start | bytes 393224 | tf_op jit(solution)/shard_map/ppermute | solution.py:675
  (145 other events, 1050.9 us)
